TPU v7x, 512 devices: a whole 4x4x16 slice. The times are simulated.
512 devices in a mesh: res: 128 (over y_lo, z, x), cx: 4 (over y_hi, core).
Axes of the slice: x: 4, y: 4 (y_hi: 2, y_lo: 2; y = y_hi * 2 + y_lo), z: 16, core: 2. Of those that a mesh axis runs over, the one named last changes fastest.
Arguments:
- homolog_representation: bfloat16 [128, 256, 256], P('cx', 'res'), parts along dimension 0, may hold values from -6 to 6
- pairwise_representation: bfloat16 [1024, 256, 128], P(('cx', 'res')), parts along dimension 0, may hold values from -6 to 6
- pairwise_refreshed_adjoint: bfloat16 [1024, 256, 128], P(('cx', 'res')), parts along dimension 0, may hold values from -6 to 6
- homolog_standard_multiplier: float32 [256], replicated, may hold values from 0.5 to 2
- pairwise_standard_multiplier: float32 [128], replicated, may hold values from 0.5 to 2
- paired_linear_operators: bfloat16 [256, 64], replicated, may hold values from -0.375 to 0.375
- closing_linear_operator: bfloat16 [1024, 128], replicated, may hold values from -0.75 to 0.75
- widening_transition_weights: bfloat16 [128, 512], replicated, may hold values from -0.5 to 0.5
- narrowing_transition_weights: bfloat16 [512, 128], replicated, may hold values from -0.25 to 0.25
Outputs:
- pair_output: bfloat16 [1024, 256, 128], P(('cx', 'res')), parts along dimension 0
- pair_gradient: bfloat16 [1024, 256, 128], P(('cx', 'res')), parts along dimension 0
- homolog_array_slope: bfloat16 [128, 256, 256], P('cx', 'res'), parts along dimension 0
- grad_out: float32 [4096, 128], P('cx'), parts along dimension 0
- projection_weight_gradient: float32 [1024, 64], P('cx'), parts along dimension 0
- grad_up: float32 [512, 512], P('cx'), parts along dimension 0
- grad_down: float32 [2048, 128], P('cx'), parts along dimension 0
There are 4 independent parts, one for each index of `cx`. A program takes and returns all parts, laid end to end along the dimension named above; an argument that names none is the same for every part. Nothing has to cross between parts.
All inputs are finite; a program needn't handle non-finite values.
Results may differ from a plain program's by a relative error of at most 0.013.
Values may be sent and summed in bfloat16 or wider, within the bound.
A program may use at most 64 MiB of HBM per device.

v0:
```python
import jax
import jax.numpy as jnp
from jax import lax
from jax.sharding import PartitionSpec as P

EPSILON = 1e-05


def centered_homolog_entries(values, norm_gain):
    center = values - jnp.mean(values, axis=-1, keepdims=True)
    spread_recip_factor = lax.rsqrt(jnp.mean(center * center, axis=-1, keepdims=True) + EPSILON)
    rescaled_homolog_entries = center * spread_recip_factor
    return (rescaled_homolog_entries * norm_gain, rescaled_homolog_entries, spread_recip_factor)


def standardize_adjoint_pass(d_normed, norm_gain, rescaled_homolog_entries, spread_recip_factor):
    d_unit = d_normed * norm_gain
    return spread_recip_factor * (
        d_unit
        - jnp.mean(d_unit, axis=-1, keepdims=True)
        - rescaled_homolog_entries
        * jnp.mean(d_unit * rescaled_homolog_entries, axis=-1, keepdims=True)
    )


def lead_dot(left_mat, right_mat):
    return lax.dot_general(
        left_mat, right_mat, (((0,), (0,)), ((), ())), preferred_element_type=jnp.float32
    )


def backward_product(values, weight):
    return lax.dot_general(
        values, weight, (((values.ndim - 1,), (1,)), ((), ())), preferred_element_type=jnp.float32
    )


def pair_row(
    left_single_row,
    right_gathered,
    pair_in,
    cot_row,
    pairwise_standard_multiplier,
    closing_linear_operator,
    widening_transition_weights,
    narrowing_transition_weights,
):
    sequence_slice = left_single_row.shape[0]
    amino_index = right_gathered.shape[1]
    projected_channels = left_single_row.shape[1]
    outer_tensor = (
        jnp.einsum(
            "nr,nxg->xrg", left_single_row, right_gathered, preferred_element_type=jnp.float32
        )
        / sequence_slice
    )
    outer_tensor = outer_tensor.reshape(
        amino_index, projected_channels * projected_channels
    ).astype(jnp.bfloat16)
    update = jnp.dot(outer_tensor, closing_linear_operator, preferred_element_type=jnp.float32)
    middle = pair_in.astype(jnp.float32) + update
    centered_operand, rescaled_homolog_entries, spread_recip_factor = centered_homolog_entries(
        middle, pairwise_standard_multiplier
    )
    centered_operand = centered_operand.astype(jnp.bfloat16)
    pre_act = jnp.dot(
        centered_operand, widening_transition_weights, preferred_element_type=jnp.float32
    )
    sigmoid_gate = jax.nn.sigmoid(pre_act)
    active = (pre_act * sigmoid_gate).astype(jnp.bfloat16)
    result = (
        middle + jnp.dot(active, narrowing_transition_weights, preferred_element_type=jnp.float32)
    ).astype(jnp.bfloat16)
    d_active = backward_product(cot_row, narrowing_transition_weights)
    d_pre = (d_active * sigmoid_gate * (1.0 + pre_act * (1.0 - sigmoid_gate))).astype(jnp.bfloat16)
    d_normed = backward_product(d_pre, widening_transition_weights)
    d_middle = (
        cot_row.astype(jnp.float32)
        + standardize_adjoint_pass(
            d_normed, pairwise_standard_multiplier, rescaled_homolog_entries, spread_recip_factor
        )
    ).astype(jnp.bfloat16)
    outer_gradient = (
        backward_product(d_middle, closing_linear_operator)
        .astype(jnp.bfloat16)
        .reshape(amino_index, projected_channels, projected_channels)
    )
    left_gradient = (
        jnp.einsum(
            "xua,dxa->du", outer_gradient, right_gathered, preferred_element_type=jnp.float32
        )
        / sequence_slice
    ).astype(jnp.bfloat16)
    row_grads = (
        lead_dot(outer_tensor, d_middle),
        lead_dot(centered_operand, d_pre),
        lead_dot(active, cot_row),
    )
    return (result, d_middle, left_gradient, outer_gradient, row_grads)


def local(
    homolog_representation,
    pairwise_representation,
    pairwise_refreshed_adjoint,
    homolog_standard_multiplier,
    pairwise_standard_multiplier,
    paired_linear_operators,
    closing_linear_operator,
    widening_transition_weights,
    narrowing_transition_weights,
):
    sequence_slice = homolog_representation.shape[0]
    local_sequences = homolog_representation.shape[1]
    amino_index = pairwise_representation.shape[1]
    projected_channels = paired_linear_operators.shape[1] // 2
    centered_operand, rescaled_homolog_entries, spread_recip_factor = centered_homolog_entries(
        homolog_representation.astype(jnp.float32), homolog_standard_multiplier
    )
    centered_operand = centered_operand.astype(jnp.bfloat16)
    flat_rows = centered_operand.reshape(-1, centered_operand.shape[-1])
    projected_rows = jnp.dot(
        flat_rows, paired_linear_operators, preferred_element_type=jnp.float32
    ).astype(jnp.bfloat16)
    projected_rows = projected_rows.reshape(sequence_slice, local_sequences, 2 * projected_channels)
    left_proj = projected_rows[..., :projected_channels]
    inputs = (jnp.swapaxes(left_proj, 0, 1), pairwise_representation, pairwise_refreshed_adjoint)
    weight_initial = (
        jnp.zeros(closing_linear_operator.shape, jnp.float32),
        jnp.zeros(widening_transition_weights.shape, jnp.float32),
        jnp.zeros(narrowing_transition_weights.shape, jnp.float32),
    )
    right_gathered = lax.all_gather(
        projected_rows[..., projected_channels:], "res", axis=1, tiled=True
    )

    def row_step(accumulated_sums, row_inputs):
        left_single_row, pair_in, cot_row = row_inputs
        result, d_middle, left_gradient, outer_gradient, row_grads = pair_row(
            left_single_row,
            right_gathered,
            pair_in,
            cot_row,
            pairwise_standard_multiplier,
            closing_linear_operator,
            widening_transition_weights,
            narrowing_transition_weights,
        )
        col_part = jnp.einsum(
            "sc,jce->sje", left_single_row, outer_gradient, preferred_element_type=jnp.float32
        )
        accumulated_sums = (
            accumulated_sums[0] + row_grads[0],
            accumulated_sums[1] + row_grads[1],
            accumulated_sums[2] + row_grads[2],
            accumulated_sums[3] + col_part,
        )
        return (accumulated_sums, (result, d_middle, left_gradient))

    initial_sums = weight_initial + (
        jnp.zeros((sequence_slice, amino_index, projected_channels), jnp.float32),
    )
    accumulated_sums, (pair_output, pair_gradient, d_lefts) = lax.scan(
        row_step, initial_sums, inputs
    )
    column_accumulated = lax.psum_scatter(
        accumulated_sums[3], "res", scatter_dimension=1, tiled=True
    )
    right_gradient = (column_accumulated / sequence_slice).astype(jnp.bfloat16)
    left_gradient = jnp.swapaxes(d_lefts, 0, 1)
    projection_gradient = jnp.concatenate([left_gradient, right_gradient], axis=-1)
    local_proj = lead_dot(flat_rows, projection_gradient.reshape(-1, 2 * projected_channels))
    homolog_standard_slope = backward_product(projection_gradient, paired_linear_operators)
    homolog_array_slope = standardize_adjoint_pass(
        homolog_standard_slope,
        homolog_standard_multiplier,
        rescaled_homolog_entries,
        spread_recip_factor,
    ).astype(jnp.bfloat16)
    grad_out, grad_up, grad_down, projection_weight_gradient = lax.psum(
        (accumulated_sums[0], accumulated_sums[1], accumulated_sums[2], local_proj), "res"
    )
    return (
        pair_output,
        pair_gradient,
        homolog_array_slope,
        grad_out / amino_index,
        projection_weight_gradient / amino_index,
        grad_up / amino_index,
        grad_down / amino_index,
    )


def solution(mesh):
    placed = (
        P("cx", "res", None),
        P(("cx", "res"), None, None),
        P(("cx", "res"), None, None),
        P(),
        P(),
        P(),
        P(),
        P(),
        P(),
    )
    return jax.shard_map(
        local,
        mesh=mesh,
        in_specs=placed,
        out_specs=(
            P(("cx", "res"), None, None),
            P(("cx", "res"), None, None),
            P("cx", "res", None),
            P("cx", None),
            P("cx", None),
            P("cx", None),
            P("cx", None),
        ),
        check_vma=False,
    )
```

profile of v0, /device:TPU:24, one launch (start us, length us, event | category | flops | bytes accessed | tf_op | source)
XLA Modules:
  0.0 2130.1 jit_solution(13630085630814476837)
XLA Ops:
  7.3 0.8 convert_reduce_fusion
  8.2 0.9 fusion.30
  9.7 0.9 fusion.25
  11.0 342.7 %all_gather.3 = bf16[32,256,32]{2,0,1:T(8,128)(2,1)} all-gather(bf16[32,2,32]{2,0,1:T(8,128)(2,1)S(1)} %copy.77), channel_id=1, replica_groups=mesh['res'=128,'cx'=4] {'res'}, dimensions={1}, use_global_device_ids=true | all-gather | bytes 528384 | tf_op jit(solution)/shard_map/all_gather | solution.py:133
  353.7 3.6 copy.57
  357.4 34.8 %while.23 = (s32[]{:T(128)}, f32[1024,128]{1,0:T(8,128)S(1)}, f32[128,512]{1,0:T(8,128)}, f32[512,128]{1,0:T(8,128)}, f32[32,256,32]{1,0,2:T(8,128)S(1)}, /*inde...) while((s32[]{:T(128)}, f32[1024,128]{1,0:T(8,128)S(1)}, ...), condition=%wide.region_7.8_spmd.clone, body=%wide.region_2.7_spmd.clone.sunk | while | flops 458328320 | bytes 17496812 | solution.py:163
  357.4 0.8 constant_dynamic-slice_fusion.5
  359.0 0.8 constant_dynamic-slice_fusion.4
  360.9 2.0 fusion.104
  362.9 1.4 fusion.107
  365.0 1.4 fusion.105
  366.4 2.1 convolution_add_fusion.12
  368.5 1.1 fusion.106
  369.7 0.9 convolution_add_fusion.11
  371.1 1.5 constant_dynamic-update-slice_fusion.5
  374.3 0.8 constant_dynamic-slice_fusion.5
  375.9 0.8 constant_dynamic-slice_fusion.4
  377.8 2.0 fusion.104
  379.8 1.4 fusion.107
  381.9 1.4 fusion.105
  383.3 2.2 convolution_add_fusion.12
  385.5 1.1 fusion.106
  386.6 1.9 convolution_add_fusion.11
  389.0 1.5 constant_dynamic-update-slice_fusion.5
  392.3 4.4 copy.61
  396.7 618.2 %reduce-scatter.2.cloned.1.call-done = f32[32,2,32]{2,0,1:T(8,128)} async-done(((f32[32,256,32]{2,0,1:T(8,128)}), f32[32,2,32]{2,0,1:T(8,128)}) %reduce-scatter.2.cloned.1.call-update) | async-done | bytes 8208 | tf_op jit(solution)/shard_map/reduce_scatter | solution.py:166
  1015.7 0.9 convolution_bitcast_fusion.1
  1017.7 1098.8 %all-reduce.3.cloned.1.call-done = (f32[1024,128]{1,0:T(8,128)}, f32[256,64]{0,1:T(8,128)}, f32[128,512]{1,0:T(8,128)}, f32[512,128]{1,0:T(8,128)}) async-done(((f32[1024,128]{1,0:T(8,128)}, f32[256,64]{0,1:T(8,128)}, f32[128,512]{1,0:T(8,128)}, f32[512,128]{1,0:T(8,128)}), (f32[1024,128]{1,0:T(8,128)}, f32[256,64]{0,1:T(8,128)}, f32[128,512]{1,0:T(8,128)}, ...) | async-done | bytes 1114128 | tf_op jit(solution)/shard_map/psum | solution.py:180
  2116.6 1.9 broadcast_multiply_fusion.3
  2118.4 1.5 broadcast_multiply_fusion.6
  2119.9 1.7 broadcast_multiply_fusion.5
  2121.6 1.7 broadcast_multiply_fusion.4
  (88 shorter events, 12.2 us)
Async XLA Ops:
  7.2 3.5 copy-start
  7.2 350.1 %copy-start.1 = (bf16[1024,128]{1,0:T(8,128)(2,1)S(1)}, bf16[1024,128]{1,0:T(8,128)(2,1)}, u32[]{:S(2)}) copy-start(bf16[1024,128]{1,0:T(8,128)(2,1)} %param.17) | copy-start | bytes 786436
  7.2 350.1 %copy-start.7 = (f32[128]{0:T(128)S(1)}, f32[128]{0:T(128)}, u32[]{:S(2)}) copy-start(f32[128]{0:T(128)} %param.15) | copy-start | bytes 1540
  7.2 1007.7 %reduce-scatter.2.cloned.1.call-start = ((), (), s32[]{:S(2)}) async-start(), calls=%async_computation.1 | async-start | bytes 4227072 | tf_op jit(solution)/shard_map/reduce_scatter | solution.py:166
  9.1 0.6 copy-start.8
  10.6 346.8 %copy-start.5 = (bf16[32,2,256]{2,0,1:T(8,128)(2,1)}, bf16[32,2,256]{2,0,1:T(8,128)(2,1)S(1)}, u32[]{:S(2)}) copy-start(bf16[32,2,256]{2,0,1:T(8,128)(2,1)S(1)} %fusion.25) | copy-start | bytes 98308
  365.0 5.6 copy-start.3
  381.9 6.6 copy-start.3
  392.2 4.5 copy-start.2
  392.2 623.5 %copy-start.6 = (bf16[32,2,256]{2,0,1:T(8,128)(2,1)S(1)}, bf16[32,2,256]{2,0,1:T(8,128)(2,1)}, u32[]{:S(2)}) copy-start(bf16[32,2,256]{2,0,1:T(8,128)(2,1)} %copy-done.5) | copy-start | bytes 98308
  392.2 624.4 %copy-start.4 = (bf16[32,2,256]{2,1,0:T(2,128)(2,1)S(1)}, bf16[32,2,256]{2,1,0:T(2,128)(2,1)}, u32[]{:S(2)}) copy-start(bf16[32,2,256]{2,1,0:T(2,128)(2,1)} %param.11) | copy-start | bytes 98308
  392.2 624.4 %copy-start.9 = (f32[32,2]{0,1:T(2,128)S(1)}, f32[32,2]{0,1:T(2,128)}, u32[]{:S(2)}) copy-start(f32[32,2]{0,1:T(2,128)} %copy-done.8) | copy-start | bytes 772
  392.3 624.4 %copy-start.10 = (f32[256]{0:T(256)S(1)}, f32[256]{0:T(256)}, u32[]{:S(2)}) copy-start(f32[256]{0:T(256)} %param.14) | copy-start | bytes 3076
  396.7 1719.9 %all-reduce.3.cloned.1.call-start = ((), (), s32[]{:S(2)}) async-start(), calls=%async_computation.2 | async-start | bytes 2228224 | tf_op jit(solution)/shard_map/psum | solution.py:180
Sparse Core Ops, SparseCore 0:
  396.8 618.0 reduce-scatter.1
  1019.0 1097.4 all-reduce.2
where the time goes:
time: 2130 us
  waiting for transfers between devices  1720 us (81%)
  blocking collectives  343 us (16%)
  matrix products  24.7 us (1%)
    psum x1, waiting for transfers between devices, local(): lax.psum((accumulated_sums[0], accumulated_sums[1], accumulated_sums[2],...  1100 us
    reduce_scatter x1, waiting for transfers between devices, local(): lax.psum_scatter(accumulated_sums[3], 'res', scatter_dimension=1, tiled=T...  618 us
    all_gather x1, blocking collectives, local(): lax.all_gather(projected_rows[..., projected_channels:], 'res', axis=1, t...  343 us
  transfers between devices with their start and end apart: 2, of which 2 were waited for; matrix products, arithmetic and copies ran while one was open for 0% of the time, Pallas kernels for 0%

commit v1 on v0

v1 whole, which is shorter than its diff:
```python
import functools

import jax
import jax.numpy as jnp
from jax import lax
from jax.experimental import pallas as pl
from jax.experimental.pallas import tpu as pltpu
from jax.sharding import PartitionSpec as P

EPSILON = 1e-05
F32 = jnp.float32
BF16 = jnp.bfloat16
MESH = pl.DeviceIdType.MESH


def dot(a, b, ca=1, cb=0):
    return lax.dot_general(a, b, (((ca,), (cb,)), ((), ())), preferred_element_type=F32)


def layer_norm_parts(values):
    center = values - jnp.mean(values, axis=-1, keepdims=True)
    scale = lax.rsqrt(jnp.mean(center * center, axis=-1, keepdims=True) + EPSILON)
    return center * scale, scale


def layer_norm_adjoint(d_normed, gain, unit, scale):
    e = d_normed * gain
    return scale * (
        e
        - jnp.mean(e, axis=-1, keepdims=True)
        - unit * jnp.mean(e * unit, axis=-1, keepdims=True)
    )


def factor_index(block):
    return (block % 4) * 8 + block // 4


def main_kernel(
    dims,
    msa_hbm, pair_hbm, cot_hbm, gm_ref, gp_ref, wp_ref, wc_hbm, ww_hbm, wn_hbm,
    pair_out_hbm, pair_grad_hbm, msa_grad_ref, weights_ref, proj_ref,
    msa, pair, cot, wc, ww, wn,
    wcf, wide, m_mat, d_act, xn, unit_m, scale_m, left, left_t,
    own, gathered, gathered_f, r_mat,
    pn, active, d_pre, g_mat, res_out, grad_out_rows, dm_wide,
    d_part, d_recv, d_mid, d_recv2,
    w_part, w_recv, w_mid, w_recv2, w_own, w_all,
    p_part, p_recv, p_mid, p_recv2, p_own, p_all,
    load_sem, store_sem, z_send, z_recv, xy_send, xy_recv,
):
    ny, nz, nx = dims
    np_ = ny * nx
    n = np_ * nz
    me = lax.axis_index("res")
    x = lax.rem(me, nx)
    z = lax.rem(me // nx, nz)
    y = me // (nx * nz)
    p = y * nx + x

    def z_device(zz):
        return {"res": (y * nz + zz) * nx + x}

    def xy_device(pp):
        return {"res": ((pp // nx) * nz + z) * nx + lax.rem(pp, nx)}

    barrier = pltpu.get_barrier_semaphore()

    @pl.loop(1, nz)
    def _(k):
        pl.semaphore_signal(barrier, inc=1, device_id=z_device(lax.rem(z + k, nz)), device_id_type=MESH)

    @pl.loop(1, np_)
    def _(k):
        pl.semaphore_signal(barrier, inc=1, device_id=xy_device(lax.rem(p + k, np_)), device_id_type=MESH)

    loads = [
        pltpu.make_async_copy(src, dst, load_sem.at[i])
        for i, (src, dst) in enumerate(
            [(msa_hbm, msa), (wc_hbm, wc), (cot_hbm, cot), (wn_hbm, wn), (ww_hbm, ww), (pair_hbm, pair)]
        )
    ]
    for load in loads:
        load.start()

    def z_copy(stage, src, dst, zz, slot):
        return pltpu.make_async_remote_copy(
            src_ref=src, dst_ref=dst, send_sem=z_send.at[stage, zz], recv_sem=z_recv.at[stage, slot],
            device_id=z_device(zz), device_id_type=MESH)

    def xy_copy(stage, src, dst, pp, slot):
        return pltpu.make_async_remote_copy(
            src_ref=src, dst_ref=dst, send_sem=xy_send.at[stage, pp], recv_sem=xy_recv.at[stage, slot],
            device_id=xy_device(pp), device_id_type=MESH)

    def z_start(stage, src, dst):
        @pl.loop(1, nz)
        def _(k):
            zz = lax.rem(z + k, nz)
            z_copy(stage, src(zz), dst(z), zz, z).start()

    def z_wait(stage, src, dst):
        @pl.loop(1, nz)
        def _(k):
            zz = lax.rem(z + k, nz)
            z_copy(stage, src(zz), dst(zz), zz, zz).wait_recv()

    def z_done(stage, src, dst):
        @pl.loop(1, nz)
        def _(k):
            zz = lax.rem(z + k, nz)
            z_copy(stage, src(zz), dst(zz), zz, zz).wait_send()

    def xy_start(stage, src, dst):
        @pl.loop(1, np_)
        def _(k):
            pp = lax.rem(p + k, np_)
            xy_copy(stage, src(pp), dst(p), pp, p).start()

    def xy_wait(stage, src, dst):
        @pl.loop(1, np_)
        def _(k):
            pp = lax.rem(p + k, np_)
            xy_copy(stage, src(pp), dst(pp), pp, pp).wait_recv()

    def xy_done(stage, src, dst):
        @pl.loop(1, np_)
        def _(k):
            pp = lax.rem(p + k, np_)
            xy_copy(stage, src(pp), dst(pp), pp, pp).wait_send()

    def slab(ref, pp):
        return ref.at[pp // nx, :, lax.rem(pp, nx)]

    zs = {
        "gather": (0, lambda zz: own, lambda s: gathered.at[y, s, x]),
        "d": (1, lambda zz: d_mid.at[zz], lambda s: d_recv2.at[s]),
        "w": (2, lambda zz: w_mid.at[zz], lambda s: w_recv2.at[s]),
        "w_all": (3, lambda zz: w_own, lambda s: w_all.at[p, s]),
        "p": (4, lambda zz: p_mid, lambda s: p_recv2.at[s]),
    }
    xys = {
        "gather": (0, lambda pp: slab(gathered, p), lambda s: slab(gathered, s)),
        "d": (1, lambda pp: slab(d_part, pp), lambda s: d_recv.at[s]),
        "w": (2, lambda pp: w_part.at[pp], lambda s: w_recv.at[s]),
        "w_all": (3, lambda pp: w_all.at[p], lambda s: w_all.at[s]),
        "p": (4, lambda pp: p_part.at[pp], lambda s: p_recv.at[s]),
        "p_all": (5, lambda pp: p_own, lambda s: p_all.at[s]),
    }

    loads[0].wait()
    rows = jnp.concatenate([msa[:, 0, :].astype(F32), msa[:, 1, :].astype(F32)], axis=0)
    unit, scale = layer_norm_parts(rows)
    unit_m[...] = unit
    scale_m[...] = jnp.broadcast_to(scale, scale_m.shape)
    normed = (unit * gm_ref[...]).astype(BF16)
    xn[...] = normed
    proj_t = dot(wp_ref[...], normed, 1, 1)
    right_t = proj_t[32:64]
    own_f = jnp.concatenate(
        [
            jnp.concatenate([right_t[t * 8 : (t + 1) * 8, b * 32 : (b + 1) * 32] for t in range(4)], axis=1)
            for b in range(2)
        ],
        axis=0,
    )
    own[...] = own_f.astype(BF16)
    gathered[y, z, x] = own_f.astype(BF16)
    pl.semaphore_wait(barrier, nz - 1 + np_ - 1)
    z_start(*zs["gather"])

    left_t[...] = proj_t[0:32].astype(BF16)
    left[...] = dot(normed, wp_ref[0:32, :], 1, 1).astype(BF16)

    z_wait(*zs["gather"])
    xy_start(*xys["gather"])

    loads[1].wait()
    wcf[...] = wc[...].astype(F32)
    for block in range(32):
        wide[:, block * 128 : (block + 1) * 128] = wcf[pl.ds(factor_index(block), 32, stride=32), :].astype(BF16)
    for block in range(32):
        part = dot(left[...], wide[:, block * 128 : (block + 1) * 128]) * (1.0 / 32.0)
        for b in range(2):
            m_mat[block * 32 : (block + 1) * 32, b * 128 : (b + 1) * 128] = part[b * 32 : (b + 1) * 32].astype(BF16)
    loads[2].wait()
    loads[3].wait()
    for b in range(2):
        d_act[b] = dot(cot[b], wn[...], 1, 1)
    loads[4].wait()
    loads[5].wait()

    xy_wait(*xys["gather"])
    gathered_f[...] = gathered[...].reshape(n * 16, 128).astype(F32)
    for q in range(8):
        r_mat[:, q * 128 : (q + 1) * 128] = gathered_f[pl.ds(q, 2 * n, stride=8), :].astype(BF16)

    update = dot(r_mat[...], m_mat[...])
    gain_p = gp_ref[...]
    for b in range(2):
        middle = pair[b].astype(F32) + update[:, b * 128 : (b + 1) * 128]
        unit, scale = layer_norm_parts(middle)
        normed = (unit * gain_p).astype(BF16)
        pn[b] = normed
        pre = dot(normed, ww[...])
        gate = jax.nn.sigmoid(pre)
        act_f = pre * gate
        act = act_f.astype(BF16)
        active[b] = act
        res_out[b] = (middle + dot(act, wn[...])).astype(BF16)
        dp = (d_act[b] * (gate + act_f * (1.0 - gate))).astype(BF16)
        d_pre[b] = dp
        d_normed = dot(dp, ww[...], 1, 1)
        grad = (cot[b].astype(F32) + layer_norm_adjoint(d_normed, gain_p, unit, scale)).astype(BF16)
        grad_out_rows[b] = grad
        g_mat[:, b * 128 : (b + 1) * 128] = grad
    stores = [
        pltpu.make_async_copy(res_out, pair_out_hbm, store_sem.at[0]),
        pltpu.make_async_copy(grad_out_rows, pair_grad_hbm, store_sem.at[1]),
    ]
    for store in stores:
        store.start()

    for q in range(8):
        gathered_f[pl.ds(q, 2 * n, stride=8), :] = dot(g_mat[...], m_mat[q * 128 : (q + 1) * 128, :], 1, 1)
    d_part[...] = gathered_f[...].astype(BF16).reshape(d_part.shape)
    xy_start(*xys["d"])

    for block in range(8):
        dm = dot(r_mat[:, block * 128 : (block + 1) * 128], g_mat[...], 0, 0)
        for i in range(4):
            for b in range(2):
                dm_wide[b * 32 : (b + 1) * 32, (block * 4 + i) * 128 : (block * 4 + i + 1) * 128] = dm[
                    i * 32 : (i + 1) * 32, b * 128 : (b + 1) * 128
                ].astype(BF16)
    wrows = w_part.shape[1] * w_part.shape[2]

    def put(start, value):
        count = value.shape[0]
        height = w_part.shape[2]
        done = 0
        while done < count:
            first = start + done
            take = min(wrows - first % wrows, count - done)
            w_part[first // wrows, first % wrows // height : (first % wrows + take) // height] = (
                value[done : done + take].astype(BF16).reshape(take // height, height, 128)
            )
            done += take

    for block in range(32):
        if block % 8 == 0:
            go = dot(left_t[...], dm_wide[:, block * 128 : (block + 8) * 128]) * (1.0 / 32.0)
            go = jnp.concatenate([go[:, i * 128 : (i + 1) * 128] for i in range(8)], axis=0)
            put(block * 32, go)
    put(1024, dot(active[0], cot[0], 0, 0) + dot(active[1], cot[1], 0, 0))
    up = dot(pn[0], d_pre[0], 0, 0) + dot(pn[1], d_pre[1], 0, 0)
    put(1536, jnp.concatenate([up[:, i * 128 : (i + 1) * 128] for i in range(4)], axis=0))
    xy_start(*xys["w"])
    d_left_t = (dot(wide[...], dm_wide[...], 1, 1) * (1.0 / 32.0)).astype(BF16)

    d_recv[p] = d_part[y, :, x]
    xy_wait(*xys["d"])
    total = d_recv[0].astype(F32)
    for i in range(1, np_):
        total += d_recv[i].astype(F32)
    d_mid[...] = total.astype(BF16)
    z_start(*zs["d"])

    w_recv[p] = w_part[p]
    xy_wait(*xys["w"])
    total = w_recv[0].astype(F32)
    for i in range(1, np_):
        total += w_recv[i].astype(F32)
    w_mid[...] = total.astype(BF16)
    z_start(*zs["w"])

    d_recv2[z] = d_mid[z]
    z_wait(*zs["d"])
    total = d_recv2[0].astype(F32)
    for i in range(1, nz):
        total += d_recv2[i].astype(F32)
    d_right_t = jnp.concatenate(
        [
            jnp.concatenate([total[b * 8 : (b + 1) * 8, t * 32 : (t + 1) * 32] for t in range(4)], axis=0)
            for b in range(2)
        ],
        axis=1,
    ).astype(BF16)
    d_proj_t = jnp.concatenate([d_left_t, d_right_t], axis=0)
    pwg = dot(d_proj_t, xn[...])
    pwg = jnp.concatenate([pwg[:, 0:128], pwg[:, 128:256]], axis=0).astype(BF16)
    p_part[...] = pwg.reshape(p_part.shape)
    xy_start(*xys["p"])

    w_recv2[z] = w_mid[z]
    z_wait(*zs["w"])
    total = w_recv2[0].astype(F32)
    for i in range(1, nz):
        total += w_recv2[i].astype(F32)
    w_own[...] = total.astype(BF16)
    w_all[p, z] = total.astype(BF16)
    z_start(*zs["w_all"])

    p_recv[p] = p_part[p]
    xy_wait(*xys["p"])
    total = p_recv[0].astype(F32)
    for i in range(1, np_):
        total += p_recv[i].astype(F32)
    p_mid[...] = total.astype(BF16)
    p_recv2[z] = total.astype(BF16)
    z_start(*zs["p"])

    z_wait(*zs["w_all"])
    xy_start(*xys["w_all"])

    d_norm = dot(d_proj_t, wp_ref[...], 0, 0)
    slope = layer_norm_adjoint(d_norm, gm_ref[...], unit_m[...], scale_m[:, 0:1])
    msa_grad_ref[...] = slope.astype(BF16)

    z_wait(*zs["p"])
    total = p_recv2[0].astype(F32)
    for i in range(1, nz):
        total += p_recv2[i].astype(F32)
    p_own[...] = total.astype(BF16)
    p_all[p] = total.astype(BF16)
    xy_start(*xys["p_all"])
    xy_wait(*xys["w_all"])
    weights_ref[...] = w_all[...].reshape(weights_ref.shape)
    xy_wait(*xys["p_all"])
    proj_ref[...] = p_all[...].reshape(proj_ref.shape)

    for plan in zs.values():
        z_done(*plan)
    for plan in xys.values():
        xy_done(*plan)
    for store in stores:
        store.wait()


def final_kernel(
    pair_in, grad_in, msa_in, weights, proj,
    pair_out, grad_out_pair, msa_out, grad_out, proj_out, grad_up, grad_down,
    sem,
):
    copies = [
        pltpu.make_async_copy(pair_in, pair_out, sem.at[0]),
        pltpu.make_async_copy(grad_in, grad_out_pair, sem.at[1]),
    ]
    for copy in copies:
        copy.start()
    inv = 1.0 / 256.0
    for b in range(2):
        msa_out[:, b, :] = msa_in[b * 32 : (b + 1) * 32, :]
    for block in range(32):
        grad_out[pl.ds(factor_index(block), 32, stride=32), :] = (
            weights[block * 32 : (block + 1) * 32, :].astype(F32) * inv
        )
    grad_down[...] = weights[1024:1536, :].astype(F32) * inv
    for i in range(4):
        grad_up[:, i * 128 : (i + 1) * 128] = weights[1536 + i * 128 : 1536 + (i + 1) * 128, :].astype(F32) * inv
    for i in range(2):
        proj_out[:, i * 128 : (i + 1) * 128] = proj[i * 64 : (i + 1) * 64, :].astype(F32) * inv
    for copy in copies:
        copy.wait()


def local(dims, msa, pair, cot, gm, gp, wp, wc, ww, wn):
    ny, nz, nx = dims
    np_ = ny * nx
    n = np_ * nz
    wh = 2048 // n
    ph = 128 // np_
    hbm = pl.BlockSpec(memory_space=pl.ANY)
    vmem = pl.BlockSpec(memory_space=pltpu.VMEM)
    rows = pair.shape[1]

    def V(shape, dtype=BF16):
        return pltpu.VMEM(shape, dtype)

    scratch = [
        V((32, 2, 256)), V((2, rows, 128)), V((2, rows, 128)), V((1024, 128)), V((128, 512)), V((512, 128)),
        V((1024, 128), F32), V((32, 4096)), V((1024, 256)), V((2, rows, 512), F32), V((64, 256)),
        V((64, 256), F32), V((64, 128), F32), V((64, 32)), V((32, 64)),
        V((16, 128)), V((ny, nz, nx, 16, 128)), V((n * 16, 128), F32), V((rows, 1024)),
        V((2, rows, 128)), V((2, rows, 512)), V((2, rows, 512)), V((rows, 256)), V((2, rows, 128)),
        V((2, rows, 128)), V((64, 4096)),
        V((ny, nz, nx, 16, 128)), V((np_, nz, 16, 128)), V((nz, 16, 128)), V((nz, 16, 128)),
        V((np_, nz, wh, 128)), V((np_, nz, wh, 128)), V((nz, wh, 128)), V((nz, wh, 128)), V((wh, 128)),
        V((np_, nz, wh, 128)),
        V((np_, ph, 128)), V((np_, ph, 128)), V((ph, 128)), V((nz, ph, 128)), V((ph, 128)), V((np_, ph, 128)),
        pltpu.SemaphoreType.DMA((6,)),
        pltpu.SemaphoreType.DMA((2,)),
        pltpu.SemaphoreType.DMA((5, nz)),
        pltpu.SemaphoreType.DMA((5, nz)),
        pltpu.SemaphoreType.DMA((6, np_)),
        pltpu.SemaphoreType.DMA((6, np_)),
    ]
    outs = pl.pallas_call(
        functools.partial(main_kernel, dims),
        out_shape=[
            jax.ShapeDtypeStruct(pair.shape, BF16),
            jax.ShapeDtypeStruct(pair.shape, BF16),
            jax.ShapeDtypeStruct((64, 256), BF16),
            jax.ShapeDtypeStruct((2048, 128), BF16),
            jax.ShapeDtypeStruct((128, 128), BF16),
        ],
        in_specs=[hbm, hbm, hbm, vmem, vmem, vmem, hbm, hbm, hbm],
        out_specs=[hbm, hbm, vmem, vmem, vmem],
        scratch_shapes=scratch,
        compiler_params=pltpu.CompilerParams(
            collective_id=0, has_side_effects=True, vmem_limit_bytes=40 * 2**20
        ),
    )(msa, pair, cot, gm.reshape(1, -1), gp.reshape(1, -1), wp.T, wc, ww, wn)
    results = pl.pallas_call(
        final_kernel,
        out_shape=[
            jax.ShapeDtypeStruct(pair.shape, BF16),
            jax.ShapeDtypeStruct(pair.shape, BF16),
            jax.ShapeDtypeStruct(msa.shape, BF16),
            jax.ShapeDtypeStruct((1024, 128), F32),
            jax.ShapeDtypeStruct((64, 256), F32),
            jax.ShapeDtypeStruct((128, 512), F32),
            jax.ShapeDtypeStruct((512, 128), F32),
        ],
        in_specs=[hbm, hbm, vmem, vmem, vmem],
        out_specs=[hbm, hbm, vmem, vmem, vmem, vmem, vmem],
        scratch_shapes=[pltpu.SemaphoreType.DMA((2,))],
        compiler_params=pltpu.CompilerParams(vmem_limit_bytes=16 * 2**20),
    )(*outs)
    return tuple(r.T if i == 4 else r for i, r in enumerate(results))


DIMS = (2, 16, 4)


def solution(mesh, dims=DIMS):
    pairs = P(("cx", "res"), None, None)
    return jax.shard_map(
        functools.partial(local, dims),
        mesh=mesh,
        in_specs=(P("cx", "res", None), pairs, pairs, P(), P(), P(), P(), P(), P()),
        out_specs=(pairs, pairs, P("cx", "res", None), P("cx", None), P("cx", None), P("cx", None), P("cx", None)),
        check_vma=False,
    )
```

time: 2130 us -> 79.2 us (0.04)
  waiting for transfers between devices: 1720 us -> 0 us
  blocking collectives: 343 us -> 0 us
  Pallas kernels: 0 us -> 71 us
  matrix products: 24.7 us -> 0 us
    psum x1 -> x0, waiting for transfers between devices: 1100 us -> none  [local(): lax.psum((accumulated_sums[0], accumulated_sums[1], accumulated_sums[2],...]
    reduce_scatter x1 -> x0, waiting for transfers between devices: 618 us -> none  [local(): lax.psum_scatter(accumulated_sums[3], 'res', scatter_dimension=1, tiled=T...]
    all_gather x1 -> x0, blocking collectives: 343 us -> none  [local(): lax.all_gather(projected_rows[..., projected_channels:], 'res', axis=1, t...]
    pallas_call x0 -> x2, Pallas kernels: none -> 71 us  [the longest x1 69.3 us: local(): pl.pallas_call(functools.partial(main_kernel, dims), out_shape=[jax.Shape...]
    dot_general x27 -> x0, matrix products: 24.7 us -> none  [the longest x7 8.67 us: lead_dot(): lax.dot_general(left_mat, right_mat, (((0,), (0,)), ((), ())), preferred_...]
  transfers between devices with their start and end apart: 2 -> 0, of which waited for: 2 -> 0; matrix products, arithmetic and copies ran while one was open for 0% -> 0% of each run, Pallas kernels for 0% -> 0%
where the time goes in v1:
time: 79.2 us; the launch traced here: 78.4 us
  Pallas kernels  71 us (90%)
  local copies, waits for them, and re-layouts  6.75 us (9%)
    pallas_call x1, Pallas kernels, local(): pl.pallas_call(functools.partial(main_kernel, dims), out_shape=[jax.Shape...  69.3 us
    unnamed x18, local copies, waits for them, and re-layouts  6.75 us
    pallas_call x1, Pallas kernels, local(): pl.pallas_call(final_kernel, out_shape=[jax.ShapeDtypeStruct(pair.shape,...  1.71 us

profile of v1, /device:TPU:24, one launch (start us, length us, event | category | flops | bytes accessed | tf_op | source)
XLA Modules:
  0.0 78.4 jit_solution(18286346205349485761)
XLA Ops:
  0.6 0.0 copy-start.7
  0.6 0.0 copy-start.8
  0.7 0.7 copy-done.7
  1.3 0.0 copy-done.8
  1.3 0.0 copy-start
  1.3 0.9 %copy-done = bf16[1024,128]{1,0:T(8,128)(2,1)S(1)} copy-done((bf16[1024,128]{1,0:T(8,128)(2,1)S(1)}, bf16[1024,128]{1,0:T(8,128)(2,1)}, u32[]{:S(2)}) %copy-start) | copy-done | bytes 262168
  2.3 0.0 copy-start.1
  2.3 0.9 %copy-done.1 = bf16[2,256,128]{2,1,0:T(8,128)(2,1)S(1)} copy-done((bf16[2,256,128]{2,1,0:T(8,128)(2,1)S(1)}, bf16[2,256,128]{2,1,0:T(8,128)(2,1)}, u32[]{:S(2)}) %copy-start.1) | copy-done | bytes 131096
  3.2 0.0 copy-start.2
  3.2 0.9 %copy-done.2 = bf16[2,256,128]{2,1,0:T(8,128)(2,1)S(1)} copy-done((bf16[2,256,128]{2,1,0:T(8,128)(2,1)S(1)}, bf16[2,256,128]{2,1,0:T(8,128)(2,1)}, u32[]{:S(2)}) %copy-start.2) | copy-done | bytes 131096
  4.1 0.0 copy-start.3
  4.1 0.9 %copy-done.3 = bf16[128,512]{1,0:T(8,128)(2,1)S(1)} copy-done((bf16[128,512]{1,0:T(8,128)(2,1)S(1)}, bf16[128,512]{1,0:T(8,128)(2,1)}, u32[]{:S(2)}) %copy-start.3) | copy-done | bytes 131096
  5.0 0.0 copy-start.4
  5.0 0.9 %copy-done.4 = bf16[512,128]{1,0:T(8,128)(2,1)S(1)} copy-done((bf16[512,128]{1,0:T(8,128)(2,1)S(1)}, bf16[512,128]{1,0:T(8,128)(2,1)}, u32[]{:S(2)}) %copy-start.4) | copy-done | bytes 131096
  5.9 0.0 copy-start.5
  5.9 0.8 copy-done.5
  6.6 0.0 copy-start.6
  6.6 0.8 copy-done.6
  7.4 69.3 %shard_map.144 = (bf16[2,256,128]{2,1,0:T(8,128)(2,1)S(1)}, bf16[2,256,128]{2,1,0:T(8,128)(2,1)S(1)}, bf16[64,256]{1,0:T(8,128)(2,1)S(1)}, bf16[2048,128]{1,0:T(8,128)(2,1)S(1)}, bf16[128,128]{1,0:T(8,128)(2,1)S(1)}) custom-call(bf16[32,2,256]{2,1,0:T(2,128)(2,1)S(1)} %copy-done.5, bf16[2,256,128]{2,1,0:T(8,128)(2,1)S(1)} %copy-done.1, ...), custom_call_target="tpu_custom_call" | custom-call | tf_op jit(solution)/shard_map/pallas_call | solution.py:398
  76.7 1.7 %shard_map.145 = (bf16[2,256,128]{2,1,0:T(8,128)(2,1)}, bf16[2,256,128]{2,1,0:T(8,128)(2,1)}, bf16[32,2,256]{2,1,0:T(2,128)(2,1)}, f32[1024,128]{1,0:T(8,128)}, ...) custom-call(bf16[2,256,128]{2,1,0:T(8,128)(2,1)S(1)} %get-tuple-element.19.pair_in, ...), custom_call_target="tpu_custom_call" | custom-call | tf_op jit(solution)/shard_map/pallas_call | solution.py:414
Async XLA Ops:
  0.6 0.7 copy-start.7
  0.6 0.7 copy-start.8
  1.3 1.0 %copy-start = (bf16[1024,128]{1,0:T(8,128)(2,1)S(1)}, bf16[1024,128]{1,0:T(8,128)(2,1)}, u32[]{:S(2)}) copy-start(bf16[1024,128]{1,0:T(8,128)(2,1)} %wc_hbm.1) | copy-start | bytes 786436
  2.3 0.9 %copy-start.1 = (bf16[2,256,128]{2,1,0:T(8,128)(2,1)S(1)}, bf16[2,256,128]{2,1,0:T(8,128)(2,1)}, u32[]{:S(2)}) copy-start(bf16[2,256,128]{2,1,0:T(8,128)(2,1)} %pair_hbm.1) | copy-start | bytes 393220
  3.2 0.9 %copy-start.2 = (bf16[2,256,128]{2,1,0:T(8,128)(2,1)S(1)}, bf16[2,256,128]{2,1,0:T(8,128)(2,1)}, u32[]{:S(2)}) copy-start(bf16[2,256,128]{2,1,0:T(8,128)(2,1)} %cot_hbm.1) | copy-start | bytes 393220
  4.1 0.9 %copy-start.3 = (bf16[128,512]{1,0:T(8,128)(2,1)S(1)}, bf16[128,512]{1,0:T(8,128)(2,1)}, u32[]{:S(2)}) copy-start(bf16[128,512]{1,0:T(8,128)(2,1)} %ww_hbm.1) | copy-start | bytes 393220
  5.0 0.9 %copy-start.4 = (bf16[512,128]{1,0:T(8,128)(2,1)S(1)}, bf16[512,128]{1,0:T(8,128)(2,1)}, u32[]{:S(2)}) copy-start(bf16[512,128]{1,0:T(8,128)(2,1)} %wn_hbm.1) | copy-start | bytes 393220
  5.9 0.8 copy-start.5
  6.6 0.8 copy-start.6

commit v2 on v1

v2 whole, which is shorter than its diff:
```python
import functools

import jax
import jax.numpy as jnp
from jax import lax
from jax.experimental import pallas as pl
from jax.experimental.pallas import tpu as pltpu
from jax.sharding import PartitionSpec as P

EPSILON = 1e-05
F32 = jnp.float32
BF16 = jnp.bfloat16
MESH = pl.DeviceIdType.MESH


def dot(a, b, ca=1, cb=0):
    return lax.dot_general(a, b, (((ca,), (cb,)), ((), ())), preferred_element_type=F32)


def layer_norm_parts(values):
    center = values - jnp.mean(values, axis=-1, keepdims=True)
    scale = lax.rsqrt(jnp.mean(center * center, axis=-1, keepdims=True) + EPSILON)
    return center * scale, scale


def layer_norm_adjoint(d_normed, gain, unit, scale):
    e = d_normed * gain
    return scale * (
        e
        - jnp.mean(e, axis=-1, keepdims=True)
        - unit * jnp.mean(e * unit, axis=-1, keepdims=True)
    )


def factor_index(block):
    return (block % 4) * 8 + block // 4


def main_kernel(
    dims,
    msa_hbm, pair_hbm, cot_hbm, gm_hbm, gp_hbm, wp_hbm, wc_hbm, ww_hbm, wn_hbm,
    res_out, grad_rows, msa_grad_ref, weights_ref, proj_ref,
    msa, gm_ref, gp_ref, wp_ref, pair, cot, wc, ww, wn,
    wcf, wide, m_mat, d_act, xn_col, unit_m, scale_m, left, left_t,
    own, gathered, flat, r_mat,
    pn, active, d_pre, g_mat, dm_wide,
    d_part, d_recv, d_mid, d_recv2,
    w_part, w_recv, w_mid, w_recv2, w_own, w_all,
    p_part, p_recv, p_mid, p_recv2, p_own, p_all,
    load_sem, z_send, z_recv, q_send, q_recv, xy_send, xy_recv, a_send, a_recv,
):
    ny, nq, nb, nx = dims
    nz = nq * nb
    np_ = ny * nx
    na = np_ * nb
    n = np_ * nz
    half = nz // 4
    me = lax.axis_index("res")
    x = lax.rem(me, nx)
    z = lax.rem(me // nx, nz)
    y = me // (nx * nz)
    q = z // nb
    b_ = lax.rem(z, nb)
    p = y * nx + x
    a = (y * nb + b_) * nx + x

    def at(yy, zz, xx):
        return {"res": (yy * nz + zz) * nx + xx}

    def z_device(zz):
        return at(y, zz, x)

    def q_device(qq):
        return at(y, qq * nb + b_, x)

    def xy_device(pp):
        return at(pp // nx, z, lax.rem(pp, nx))

    def a_device(aa):
        return at(aa // (nb * nx), q * nb + lax.rem(aa // nx, nb), lax.rem(aa, nx))

    loads = [
        pltpu.make_async_copy(src, dst, load_sem.at[i])
        for i, (src, dst) in enumerate(
            [
                (msa_hbm, msa), (gm_hbm, gm_ref), (wp_hbm, wp_ref), (wc_hbm, wc), (cot_hbm, cot),
                (wn_hbm, wn), (ww_hbm, ww), (pair_hbm, pair), (gp_hbm, gp_ref),
            ]
        )
    ]
    for load in loads[0:3]:
        load.start()

    def far_first(i):
        return lax.rem(z + nz // 2 + (1 - 2 * lax.rem(i, 2)) * ((i + 1) // 2), nz)

    barrier = pltpu.get_barrier_semaphore()

    @pl.loop(0, nz - 1)
    def _(i):
        pl.semaphore_signal(barrier, inc=1, device_id=z_device(far_first(i)), device_id_type=MESH)

    @pl.loop(1, np_)
    def _(k):
        pl.semaphore_signal(barrier, inc=1, device_id=xy_device(lax.rem(p + k, np_)), device_id_type=MESH)

    for load in loads[3:]:
        load.start()

    class Exchange:
        def __init__(self, axis, stage, src, dst):
            self.stage, self.src, self.dst = stage, src, dst
            self.device, self.count, self.mine, self.send, self.recv, self.peer = {
                "z": (z_device, nz, z, z_send, z_recv, lambda i: far_first(i - 1)),
                "q": (q_device, nq, q, q_send, q_recv, lambda i: lax.rem(q + i, nq)),
                "xy": (xy_device, np_, p, xy_send, xy_recv, lambda i: lax.rem(p + i, np_)),
                "a": (a_device, na, a, a_send, a_recv, lambda i: lax.rem(a + i, na)),
            }[axis]
            plans.append(self)

        def copy(self, to, slot, dst):
            return pltpu.make_async_remote_copy(
                src_ref=self.src(to), dst_ref=dst,
                send_sem=self.send.at[self.stage, to], recv_sem=self.recv.at[self.stage, slot],
                device_id=self.device(to), device_id_type=MESH)

        def start(self):
            @pl.loop(1, self.count)
            def _(i):
                to = self.peer(i)
                self.copy(to, self.mine, self.dst(to, self.mine)).start()

        def wait(self, first=1, last=None):
            @pl.loop(first, self.count if last is None else last)
            def _(i):
                slot = self.peer(i)
                self.copy(slot, slot, self.dst(self.mine, slot)).wait_recv()

        def done(self):
            @pl.loop(1, self.count)
            def _(i):
                to = self.peer(i)
                self.copy(to, to, self.dst(self.mine, to)).wait_send()

    plans = []

    def slot_of(at_z, from_z):
        return lax.rem(from_z - at_z + half + nz, nz)

    near = 2 * half + 1
    x_z = Exchange("z", 0, lambda to: own, lambda at_z, s: gathered.at[y, slot_of(at_z, s), x])
    x_near = Exchange(
        "xy", 0, lambda to: gathered.at[y, 0:near, x],
        lambda _, s: gathered.at[s // nx, 0:near, lax.rem(s, nx)])
    x_far = Exchange(
        "xy", 1, lambda to: gathered.at[y, near:nz, x],
        lambda _, s: gathered.at[s // nx, near:nz, lax.rem(s, nx)])
    x_norm = Exchange("q", 0, lambda to: xn_col.at[q], lambda _, s: xn_col.at[s])
    x_d = Exchange(
        "a", 0, lambda to: d_part.at[to // (nb * nx), :, lax.rem(to // nx, nb), lax.rem(to, nx)],
        lambda _, s: d_recv.at[s])
    x_d2 = Exchange("q", 1, lambda to: d_mid.at[to], lambda _, s: d_recv2.at[s])
    x_w = Exchange("a", 1, lambda to: w_part.at[to], lambda _, s: w_recv.at[s])
    x_w2 = Exchange("q", 2, lambda to: w_mid, lambda _, s: w_recv2.at[s])
    x_w3 = Exchange("a", 2, lambda to: w_own, lambda _, s: w_all.at[s])
    x_p = Exchange("xy", 2, lambda to: p_part.at[to], lambda _, s: p_recv.at[s])
    x_p2 = Exchange("z", 1, lambda to: p_mid, lambda _, s: p_recv2.at[s])
    x_p3 = Exchange("xy", 3, lambda to: p_own, lambda _, s: p_all.at[s])

    def summed(ref, count):
        total = ref[0].astype(F32)
        for i in range(1, count):
            total += ref[i].astype(F32)
        return total

    for load in loads[0:3]:
        load.wait()
    rows = jnp.concatenate([msa[:, 0, :].astype(F32), msa[:, 1, :].astype(F32)], axis=0)
    unit, scale = layer_norm_parts(rows)
    unit_m[...] = unit
    scale_m[...] = jnp.broadcast_to(scale, scale_m.shape)
    normed = (unit * gm_ref[...]).astype(BF16)
    proj_t = dot(wp_ref[...], normed, 1, 1)
    right_t = proj_t[32:64]
    own_f = jnp.concatenate(
        [
            jnp.concatenate([right_t[t * 8 : (t + 1) * 8, b * 32 : (b + 1) * 32] for t in range(4)], axis=1)
            for b in range(2)
        ],
        axis=0,
    )
    own[...] = own_f.astype(BF16)
    xn_col[q] = normed
    pl.semaphore_wait(barrier, nz - 1 + np_ - 1)
    x_z.start()
    x_norm.start()

    gathered[y, half, x] = own_f.astype(BF16)
    left_t[...] = proj_t[0:32].astype(BF16)
    left[...] = dot(normed, wp_ref[0:32, :], 1, 1).astype(BF16)
    loads[3].wait()
    wcf[...] = wc[...].astype(F32)
    for block in range(32):
        wide[:, block * 128 : (block + 1) * 128] = wcf[pl.ds(factor_index(block), 32, stride=32), :].astype(BF16)
    for block in range(32):
        part = dot(left[...], wide[:, block * 128 : (block + 1) * 128]) * (1.0 / 32.0)
        for b in range(2):
            m_mat[block * 32 : (block + 1) * 32, b * 128 : (b + 1) * 128] = part[b * 32 : (b + 1) * 32].astype(BF16)

    x_z.wait(nz - 2 * half)
    x_near.start()
    loads[4].wait()
    loads[5].wait()
    for b in range(2):
        d_act[b] = dot(cot[b], wn[...], 1, 1)
    for load in loads[6:9]:
        load.wait()
    x_z.wait(1, nz - 2 * half)
    x_far.start()

    x_near.wait()
    x_far.wait()
    for zz in range(nz):
        block = gathered[:, pl.ds(slot_of(z, zz), 1)]
        for yy in range(ny):
            flat[pl.ds((yy * nz + zz) * nx * 16, nx * 16), :] = block[yy].reshape(nx * 16, 128).astype(F32)
    for g in range(8):
        r_mat[:, g * 128 : (g + 1) * 128] = flat[pl.ds(g, 2 * n, stride=8), :].astype(BF16)

    update = dot(r_mat[...], m_mat[...])
    gain_p = gp_ref[...]
    for b in range(2):
        middle = pair[b].astype(F32) + update[:, b * 128 : (b + 1) * 128]
        unit, scale = layer_norm_parts(middle)
        normed = (unit * gain_p).astype(BF16)
        pn[b] = normed
        pre = dot(normed, ww[...])
        gate = jax.nn.sigmoid(pre)
        act_f = pre * gate
        act = act_f.astype(BF16)
        active[b] = act
        res_out[b] = (middle + dot(act, wn[...])).astype(BF16)
        dp = (d_act[b] * (gate + act_f * (1.0 - gate))).astype(BF16)
        d_pre[b] = dp
        d_normed = dot(dp, ww[...], 1, 1)
        grad = (cot[b].astype(F32) + layer_norm_adjoint(d_normed, gain_p, unit, scale)).astype(BF16)
        grad_rows[b] = grad
        g_mat[:, b * 128 : (b + 1) * 128] = grad

    for g in range(8):
        flat[pl.ds(g, 2 * n, stride=8), :] = dot(g_mat[...], m_mat[g * 128 : (g + 1) * 128, :], 1, 1)
    d_part[...] = flat[...].astype(BF16).reshape(d_part.shape)
    x_d.start()

    for block in range(8):
        dm = dot(r_mat[:, block * 128 : (block + 1) * 128], g_mat[...], 0, 0)
        for i in range(4):
            for b in range(2):
                dm_wide[b * 32 : (b + 1) * 32, (block * 4 + i) * 128 : (block * 4 + i + 1) * 128] = dm[
                    i * 32 : (i + 1) * 32, b * 128 : (b + 1) * 128
                ].astype(BF16)
    height = w_part.shape[1]

    def put(first, value):
        for i in range(0, value.shape[0], 32):
            piece, row = divmod(first + i, height)
            w_part[piece, row : row + 32] = value[i : i + 32].astype(BF16)

    for block in range(4):
        go = dot(left_t[...], dm_wide[:, block * 1024 : (block + 1) * 1024]) * (1.0 / 32.0)
        for i in range(8):
            put((block * 8 + i) * 32, go[:, i * 128 : (i + 1) * 128])
    put(1024, dot(active[0], cot[0], 0, 0) + dot(active[1], cot[1], 0, 0))
    up = dot(pn[0], d_pre[0], 0, 0) + dot(pn[1], d_pre[1], 0, 0)
    for i in range(4):
        put(1536 + i * 128, up[:, i * 128 : (i + 1) * 128])
    x_w.start()
    d_left_t = (dot(wide[...], dm_wide[...], 1, 1) * (1.0 / 32.0)).astype(BF16)
    p_left = dot(d_left_t, xn_col[q])

    def transposed(block):
        return jnp.concatenate(
            [
                jnp.concatenate([block[b * 8 : (b + 1) * 8, t * 32 : (t + 1) * 32] for t in range(4)], axis=0)
                for b in range(2)
            ],
            axis=1,
        ).astype(BF16)

    x_norm.wait()
    d_recv[a] = d_part[y, :, b_, x]
    x_d.wait()
    total = summed(d_recv, na)
    d_mid[...] = total.astype(BF16)
    x_d2.start()
    p_right = dot(transposed(total[0]), xn_col[0])
    for i in range(1, nq):
        p_right += dot(transposed(total[i]), xn_col[i])
    pwg = jnp.concatenate([p_left, p_right], axis=0)
    pwg = jnp.concatenate([pwg[:, 0:128], pwg[:, 128:256]], axis=0).astype(BF16)
    p_part[...] = pwg.reshape(p_part.shape)
    x_p.start()

    w_recv[a] = w_part[a]
    x_w.wait()
    total = summed(w_recv, na).astype(BF16)
    w_mid[...] = total
    x_w2.start()
    w_recv2[q] = total

    p_recv[p] = p_part[p]
    x_p.wait()
    total = summed(p_recv, np_).astype(BF16)
    p_mid[...] = total
    x_p2.start()
    p_recv2[z] = total

    x_w2.wait()
    total = summed(w_recv2, nq).astype(BF16)
    w_own[...] = total
    x_w3.start()
    w_all[a] = total

    d_recv2[q] = d_mid[q]
    x_d2.wait()
    d_proj_t = jnp.concatenate([d_left_t, transposed(summed(d_recv2, nq))], axis=0)
    d_norm = dot(d_proj_t, wp_ref[...], 0, 0)
    slope = layer_norm_adjoint(d_norm, gm_ref[...], unit_m[...], scale_m[:, 0:1])
    msa_grad_ref[...] = slope.astype(BF16)

    x_p2.wait()
    total = summed(p_recv2, nz).astype(BF16)
    p_own[...] = total
    x_p3.start()
    p_all[p] = total
    x_w3.wait()
    weights_ref[...] = w_all[...].reshape(weights_ref.shape)
    x_p3.wait()
    proj_ref[...] = p_all[...].reshape(proj_ref.shape)

    for plan in plans:
        plan.done()


def final_kernel(
    pair_in, grad_in, msa_in, weights, proj,
    pair_out, grad_out_pair, msa_out, grad_out, proj_out, grad_up, grad_down,
    sem,
):
    copies = [
        pltpu.make_async_copy(pair_in, pair_out, sem.at[0]),
        pltpu.make_async_copy(grad_in, grad_out_pair, sem.at[1]),
    ]
    for copy in copies:
        copy.start()
    inv = 1.0 / 256.0
    for b in range(2):
        msa_out[:, b, :] = msa_in[b * 32 : (b + 1) * 32, :]
    for block in range(32):
        grad_out[pl.ds(factor_index(block), 32, stride=32), :] = (
            weights[block * 32 : (block + 1) * 32, :].astype(F32) * inv
        )
    grad_down[...] = weights[1024:1536, :].astype(F32) * inv
    for i in range(4):
        grad_up[:, i * 128 : (i + 1) * 128] = weights[1536 + i * 128 : 1536 + (i + 1) * 128, :].astype(F32) * inv
    for i in range(2):
        proj_out[:, i * 128 : (i + 1) * 128] = proj[i * 64 : (i + 1) * 64, :].astype(F32) * inv
    for copy in copies:
        copy.wait()


def local(dims, msa, pair, cot, gm, gp, wp, wc, ww, wn):
    ny, nq, nb, nx = dims
    nz = nq * nb
    np_ = ny * nx
    na = np_ * nb
    n = np_ * nz
    wh = 2048 // na
    ph = 128 // np_
    hbm = pl.BlockSpec(memory_space=pltpu.HBM)
    vmem = pl.BlockSpec(memory_space=pltpu.VMEM)
    rows = pair.shape[1]

    def V(shape, dtype=BF16):
        return pltpu.VMEM(shape, dtype)

    D = pltpu.SemaphoreType.DMA
    scratch = [
        V((32, 2, 256)), V((1, 256), F32), V((1, 128), F32), V((64, 256)),
        V((2, rows, 128)), V((2, rows, 128)), V((1024, 128)), V((128, 512)), V((512, 128)),
        V((1024, 128), F32), V((32, 4096)), V((1024, 256)), V((2, rows, 512), F32), V((nq, 64, 256)),
        V((64, 256), F32), V((64, 128), F32), V((64, 32)), V((32, 64)),
        V((16, 128)), V((ny, nz, nx, 16, 128)), V((n * 16, 128), F32), V((rows, 1024)),
        V((2, rows, 128)), V((2, rows, 512)), V((2, rows, 512)), V((rows, 256)), V((64, 4096)),
        V((ny, nq, nb, nx, 16, 128)), V((na, nq, 16, 128)), V((nq, 16, 128)), V((nq, 16, 128)),
        V((na, wh, 128)), V((na, wh, 128)), V((wh, 128)), V((nq, wh, 128)), V((wh, 128)), V((na, wh, 128)),
        V((np_, ph, 128)), V((np_, ph, 128)), V((ph, 128)), V((nz, ph, 128)), V((ph, 128)), V((np_, ph, 128)),
        D((9,)), D((2, nz)), D((2, nz)), D((3, nq)), D((3, nq)), D((4, np_)), D((4, np_)), D((3, na)), D((3, na)),
    ]
    outs = pl.pallas_call(
        functools.partial(main_kernel, dims),
        out_shape=[
            jax.ShapeDtypeStruct(pair.shape, BF16),
            jax.ShapeDtypeStruct(pair.shape, BF16),
            jax.ShapeDtypeStruct((64, 256), BF16),
            jax.ShapeDtypeStruct((2048, 128), BF16),
            jax.ShapeDtypeStruct((128, 128), BF16),
        ],
        in_specs=[hbm] * 9,
        out_specs=[vmem] * 5,
        scratch_shapes=scratch,
        compiler_params=pltpu.CompilerParams(
            collective_id=0, has_side_effects=True, vmem_limit_bytes=40 * 2**20
        ),
    )(*[
        pltpu.with_memory_space_constraint(v, pltpu.HBM)
        for v in (msa, pair, cot, gm.reshape(1, -1), gp.reshape(1, -1), wp.T, wc, ww, wn)
    ])
    results = pl.pallas_call(
        final_kernel,
        out_shape=[
            jax.ShapeDtypeStruct(pair.shape, BF16),
            jax.ShapeDtypeStruct(pair.shape, BF16),
            jax.ShapeDtypeStruct(msa.shape, BF16),
            jax.ShapeDtypeStruct((1024, 128), F32),
            jax.ShapeDtypeStruct((64, 256), F32),
            jax.ShapeDtypeStruct((128, 512), F32),
            jax.ShapeDtypeStruct((512, 128), F32),
        ],
        in_specs=[vmem] * 5,
        out_specs=[pl.BlockSpec(memory_space=pltpu.HBM)] * 2 + [vmem] * 5,
        scratch_shapes=[pltpu.SemaphoreType.DMA((2,))],
        compiler_params=pltpu.CompilerParams(vmem_limit_bytes=16 * 2**20),
    )(*outs)
    return tuple(r.T if i == 4 else r for i, r in enumerate(results))


DIMS = (2, 4, 4, 4)


def solution(mesh, dims=DIMS):
    pairs = P(("cx", "res"), None, None)
    return jax.shard_map(
        functools.partial(local, dims),
        mesh=mesh,
        in_specs=(P("cx", "res", None), pairs, pairs, P(), P(), P(), P(), P(), P()),
        out_specs=(pairs, pairs, P("cx", "res", None), P("cx", None), P("cx", None), P("cx", None), P("cx", None)),
        check_vma=False,
    )
```

time: 79.2 us -> 81.4 us (1.028)
  Pallas kernels: 71 us -> 80.2 us
  local copies, waits for them, and re-layouts: 6.75 us -> 0 us
    pallas_call x1, Pallas kernels: 69.3 us -> 78.5 us  [local(): pl.pallas_call(functools.partial(main_kernel, dims), out_shape=[jax.Shape...]
    unnamed x18 -> x0, local copies, waits for them, and re-layouts: 6.75 us -> none
where the time goes in v2:
time: 81.4 us; the launch traced here: 80.8 us
  Pallas kernels  80.2 us (99%)
    pallas_call x1, Pallas kernels, local(): pl.pallas_call(functools.partial(main_kernel, dims), out_shape=[jax.Shape...  78.5 us
    pallas_call x1, Pallas kernels, local(): pl.pallas_call(final_kernel, out_shape=[jax.ShapeDtypeStruct(pair.shape,...  1.71 us

profile of v2, /device:TPU:24, one launch (start us, length us, event | category | flops | bytes accessed | tf_op | source)
XLA Modules:
  0.0 80.8 jit_solution(9573489419580085419)
XLA Ops:
  0.6 78.5 %shard_map.144 = (bf16[2,256,128]{2,1,0:T(8,128)(2,1)S(1)}, bf16[2,256,128]{2,1,0:T(8,128)(2,1)S(1)}, bf16[64,256]{1,0:T(8,128)(2,1)S(1)}, bf16[2048,128]{1,0:T(8,128)(2,1)S(1)}, bf16[128,128]{1,0:T(8,128)(2,1)S(1)}) custom-call(bf16[32,2,256]{2,1,0:T(2,128)(2,1)} %msa_hbm.1, bf16[2,256,128]{2,1,0:T(8,128)(2,1)} %pair_hbm.1, bf16[2,256,128]{2,1,0:T(8,128)(2,1)} %cot_hbm.1, ...), custom_call_target="tpu_custom_call" | custom-call | tf_op jit(solution)/shard_map/pallas_call | solution.py:400
  79.1 1.7 %shard_map.145 = (bf16[2,256,128]{2,1,0:T(8,128)(2,1)}, bf16[2,256,128]{2,1,0:T(8,128)(2,1)}, bf16[32,2,256]{2,1,0:T(2,128)(2,1)}, f32[1024,128]{1,0:T(8,128)}, ...) custom-call(bf16[2,256,128]{2,1,0:T(8,128)(2,1)S(1)} %get-tuple-element.19.pair_in, ...), custom_call_target="tpu_custom_call" | custom-call | tf_op jit(solution)/shard_map/pallas_call | solution.py:419

commit v3 on v2

--- a/solution.py
+++ b/solution.py
@@ -41,28 +41,23 @@
     msa_hbm, pair_hbm, cot_hbm, gm_hbm, gp_hbm, wp_hbm, wc_hbm, ww_hbm, wn_hbm,
     res_out, grad_rows, msa_grad_ref, weights_ref, proj_ref,
     msa, gm_ref, gp_ref, wp_ref, pair, cot, wc, ww, wn,
-    wcf, wide, m_mat, d_act, xn_col, unit_m, scale_m, left, left_t,
+    wcf, wide, m_mat, d_act, xn, unit_m, scale_m, left, left_t,
     own, gathered, flat, r_mat,
     pn, active, d_pre, g_mat, dm_wide,
     d_part, d_recv, d_mid, d_recv2,
     w_part, w_recv, w_mid, w_recv2, w_own, w_all,
     p_part, p_recv, p_mid, p_recv2, p_own, p_all,
-    load_sem, z_send, z_recv, q_send, q_recv, xy_send, xy_recv, a_send, a_recv,
+    load_sem, z_send, z_recv, xy_send, xy_recv,
 ):
-    ny, nq, nb, nx = dims
-    nz = nq * nb
+    ny, nz, nx = dims
     np_ = ny * nx
-    na = np_ * nb
     n = np_ * nz
     half = nz // 4
     me = lax.axis_index("res")
     x = lax.rem(me, nx)
     z = lax.rem(me // nx, nz)
     y = me // (nx * nz)
-    q = z // nb
-    b_ = lax.rem(z, nb)
     p = y * nx + x
-    a = (y * nb + b_) * nx + x
 
     def at(yy, zz, xx):
         return {"res": (yy * nz + zz) * nx + xx}
@@ -70,14 +65,8 @@
     def z_device(zz):
         return at(y, zz, x)
 
-    def q_device(qq):
-        return at(y, qq * nb + b_, x)
-
     def xy_device(pp):
         return at(pp // nx, z, lax.rem(pp, nx))
-
-    def a_device(aa):
-        return at(aa // (nb * nx), q * nb + lax.rem(aa // nx, nb), lax.rem(aa, nx))
 
     loads = [
         pltpu.make_async_copy(src, dst, load_sem.at[i])
@@ -112,11 +101,8 @@
             self.stage, self.src, self.dst = stage, src, dst
             self.device, self.count, self.mine, self.send, self.recv, self.peer = {
                 "z": (z_device, nz, z, z_send, z_recv, lambda i: far_first(i - 1)),
-                "q": (q_device, nq, q, q_send, q_recv, lambda i: lax.rem(q + i, nq)),
                 "xy": (xy_device, np_, p, xy_send, xy_recv, lambda i: lax.rem(p + i, np_)),
-                "a": (a_device, na, a, a_send, a_recv, lambda i: lax.rem(a + i, na)),
             }[axis]
-            plans.append(self)
 
         def copy(self, to, slot, dst):
             return pltpu.make_async_remote_copy(
@@ -141,8 +127,6 @@
             def _(i):
                 to = self.peer(i)
                 self.copy(to, to, self.dst(self.mine, to)).wait_send()
-
-    plans = []
 
     def slot_of(at_z, from_z):
         return lax.rem(from_z - at_z + half + nz, nz)
@@ -155,17 +139,16 @@
     x_far = Exchange(
         "xy", 1, lambda to: gathered.at[y, near:nz, x],
         lambda _, s: gathered.at[s // nx, near:nz, lax.rem(s, nx)])
-    x_norm = Exchange("q", 0, lambda to: xn_col.at[q], lambda _, s: xn_col.at[s])
-    x_d = Exchange(
-        "a", 0, lambda to: d_part.at[to // (nb * nx), :, lax.rem(to // nx, nb), lax.rem(to, nx)],
-        lambda _, s: d_recv.at[s])
-    x_d2 = Exchange("q", 1, lambda to: d_mid.at[to], lambda _, s: d_recv2.at[s])
-    x_w = Exchange("a", 1, lambda to: w_part.at[to], lambda _, s: w_recv.at[s])
-    x_w2 = Exchange("q", 2, lambda to: w_mid, lambda _, s: w_recv2.at[s])
-    x_w3 = Exchange("a", 2, lambda to: w_own, lambda _, s: w_all.at[s])
-    x_p = Exchange("xy", 2, lambda to: p_part.at[to], lambda _, s: p_recv.at[s])
-    x_p2 = Exchange("z", 1, lambda to: p_mid, lambda _, s: p_recv2.at[s])
-    x_p3 = Exchange("xy", 3, lambda to: p_own, lambda _, s: p_all.at[s])
+    x_d = Exchange("xy", 2, lambda to: d_part.at[to // nx, :, lax.rem(to, nx)], lambda _, s: d_recv.at[s])
+    x_d2 = Exchange("z", 1, lambda to: d_mid.at[to], lambda _, s: d_recv2.at[s])
+    x_w = Exchange("xy", 3, lambda to: w_part.at[to], lambda _, s: w_recv.at[s])
+    x_w2 = Exchange("z", 2, lambda to: w_mid.at[to], lambda _, s: w_recv2.at[s])
+    x_w3 = Exchange("z", 3, lambda to: w_own, lambda at_z, s: w_all.at[p, slot_of(at_z, s)])
+    x_w_near = Exchange("xy", 4, lambda to: w_all.at[p, 0:near], lambda _, s: w_all.at[s, 0:near])
+    x_w_far = Exchange("xy", 5, lambda to: w_all.at[p, near:nz], lambda _, s: w_all.at[s, near:nz])
+    x_p = Exchange("xy", 6, lambda to: p_part.at[to], lambda _, s: p_recv.at[s])
+    x_p2 = Exchange("z", 4, lambda to: p_mid, lambda _, s: p_recv2.at[s])
+    x_p3 = Exchange("xy", 7, lambda to: p_own, lambda _, s: p_all.at[s])
 
     def summed(ref, count):
         total = ref[0].astype(F32)
@@ -190,10 +173,9 @@
         axis=0,
     )
     own[...] = own_f.astype(BF16)
-    xn_col[q] = normed
+    xn[...] = normed
     pl.semaphore_wait(barrier, nz - 1 + np_ - 1)
     x_z.start()
-    x_norm.start()
 
     gathered[y, half, x] = own_f.astype(BF16)
     left_t[...] = proj_t[0:32].astype(BF16)
@@ -259,12 +241,12 @@
                 dm_wide[b * 32 : (b + 1) * 32, (block * 4 + i) * 128 : (block * 4 + i + 1) * 128] = dm[
                     i * 32 : (i + 1) * 32, b * 128 : (b + 1) * 128
                 ].astype(BF16)
-    height = w_part.shape[1]
+    slab, height = w_part.shape[1] * w_part.shape[2], w_part.shape[2]
 
     def put(first, value):
-        for i in range(0, value.shape[0], 32):
-            piece, row = divmod(first + i, height)
-            w_part[piece, row : row + 32] = value[i : i + 32].astype(BF16)
+        for i in range(0, value.shape[0], 16):
+            peer, row = divmod(first + i, slab)
+            w_part[peer, row // height, row % height : row % height + 16] = value[i : i + 16].astype(BF16)
 
     for block in range(4):
         go = dot(left_t[...], dm_wide[:, block * 1024 : (block + 1) * 1024]) * (1.0 / 32.0)
@@ -274,9 +256,7 @@
     up = dot(pn[0], d_pre[0], 0, 0) + dot(pn[1], d_pre[1], 0, 0)
     for i in range(4):
         put(1536 + i * 128, up[:, i * 128 : (i + 1) * 128])
-    x_w.start()
     d_left_t = (dot(wide[...], dm_wide[...], 1, 1) * (1.0 / 32.0)).astype(BF16)
-    p_left = dot(d_left_t, xn_col[q])
 
     def transposed(block):
         return jnp.concatenate(
@@ -287,58 +267,67 @@
             axis=1,
         ).astype(BF16)
 
-    x_norm.wait()
-    d_recv[a] = d_part[y, :, b_, x]
+    d_recv[p] = d_part[y, :, x]
+    w_recv[p] = w_part[p]
     x_d.wait()
-    total = summed(d_recv, na)
-    d_mid[...] = total.astype(BF16)
+    total = summed(d_recv, np_).astype(BF16)
+    d_mid[...] = total
     x_d2.start()
-    p_right = dot(transposed(total[0]), xn_col[0])
-    for i in range(1, nq):
-        p_right += dot(transposed(total[i]), xn_col[i])
-    pwg = jnp.concatenate([p_left, p_right], axis=0)
+    x_w.start()
+    d_recv2[z] = d_mid[z]
+
+    x_w.wait()
+    w_mid[...] = summed(w_recv, np_).astype(BF16)
+    x_w2.start()
+    w_recv2[z] = w_mid[z]
+
+    x_d2.wait()
+    d_proj_t = jnp.concatenate([d_left_t, transposed(summed(d_recv2, nz))], axis=0)
+    pwg = dot(d_proj_t, xn[...])
     pwg = jnp.concatenate([pwg[:, 0:128], pwg[:, 128:256]], axis=0).astype(BF16)
     p_part[...] = pwg.reshape(p_part.shape)
     x_p.start()
-
-    w_recv[a] = w_part[a]
-    x_w.wait()
-    total = summed(w_recv, na).astype(BF16)
-    w_mid[...] = total
-    x_w2.start()
-    w_recv2[q] = total
-
     p_recv[p] = p_part[p]
+    d_norm = dot(d_proj_t, wp_ref[...], 0, 0)
+    slope = layer_norm_adjoint(d_norm, gm_ref[...], unit_m[...], scale_m[:, 0:1])
+    msa_grad_ref[...] = slope.astype(BF16)
+
     x_p.wait()
     total = summed(p_recv, np_).astype(BF16)
     p_mid[...] = total
     x_p2.start()
     p_recv2[z] = total
 
+    for plan in (x_z, x_near, x_far, x_d, x_w):
+        plan.done()
+
     x_w2.wait()
-    total = summed(w_recv2, nq).astype(BF16)
+    total = summed(w_recv2, nz).astype(BF16)
     w_own[...] = total
     x_w3.start()
-    w_all[a] = total
-
-    d_recv2[q] = d_mid[q]
-    x_d2.wait()
-    d_proj_t = jnp.concatenate([d_left_t, transposed(summed(d_recv2, nq))], axis=0)
-    d_norm = dot(d_proj_t, wp_ref[...], 0, 0)
-    slope = layer_norm_adjoint(d_norm, gm_ref[...], unit_m[...], scale_m[:, 0:1])
-    msa_grad_ref[...] = slope.astype(BF16)
-
+    w_all[p, half] = total
+
+    x_w3.wait(nz - 2 * half)
+    x_w_near.start()
     x_p2.wait()
     total = summed(p_recv2, nz).astype(BF16)
     p_own[...] = total
     x_p3.start()
     p_all[p] = total
-    x_w3.wait()
-    weights_ref[...] = w_all[...].reshape(weights_ref.shape)
+    x_w3.wait(1, nz - 2 * half)
+    x_w_far.start()
+    for plan in (x_d2, x_p, x_w2, x_p2, x_w3):
+        plan.done()
     x_p3.wait()
     proj_ref[...] = p_all[...].reshape(proj_ref.shape)
-
-    for plan in plans:
+    x_w_near.wait()
+    x_w_far.wait()
+    for zz in range(nz):
+        block = w_all[:, pl.ds(slot_of(z, zz), 1)]
+        for pp in range(np_):
+            weights_ref[pl.ds((pp * nz + zz) * height, height), :] = block[pp, 0]
+
+    for plan in (x_p3, x_w_near, x_w_far):
         plan.done()
 
 
@@ -370,12 +359,10 @@
 
 
 def local(dims, msa, pair, cot, gm, gp, wp, wc, ww, wn):
-    ny, nq, nb, nx = dims
-    nz = nq * nb
+    ny, nz, nx = dims
     np_ = ny * nx
-    na = np_ * nb
     n = np_ * nz
-    wh = 2048 // na
+    wh = 2048 // n
     ph = 128 // np_
     hbm = pl.BlockSpec(memory_space=pltpu.HBM)
     vmem = pl.BlockSpec(memory_space=pltpu.VMEM)
@@ -388,14 +375,15 @@
     scratch = [
         V((32, 2, 256)), V((1, 256), F32), V((1, 128), F32), V((64, 256)),
         V((2, rows, 128)), V((2, rows, 128)), V((1024, 128)), V((128, 512)), V((512, 128)),
-        V((1024, 128), F32), V((32, 4096)), V((1024, 256)), V((2, rows, 512), F32), V((nq, 64, 256)),
+        V((1024, 128), F32), V((32, 4096)), V((1024, 256)), V((2, rows, 512), F32), V((64, 256)),
         V((64, 256), F32), V((64, 128), F32), V((64, 32)), V((32, 64)),
         V((16, 128)), V((ny, nz, nx, 16, 128)), V((n * 16, 128), F32), V((rows, 1024)),
         V((2, rows, 128)), V((2, rows, 512)), V((2, rows, 512)), V((rows, 256)), V((64, 4096)),
-        V((ny, nq, nb, nx, 16, 128)), V((na, nq, 16, 128)), V((nq, 16, 128)), V((nq, 16, 128)),
-        V((na, wh, 128)), V((na, wh, 128)), V((wh, 128)), V((nq, wh, 128)), V((wh, 128)), V((na, wh, 128)),
+        V((ny, nz, nx, 16, 128)), V((np_, nz, 16, 128)), V((nz, 16, 128)), V((nz, 16, 128)),
+        V((np_, nz, wh, 128)), V((np_, nz, wh, 128)), V((nz, wh, 128)), V((nz, wh, 128)), V((wh, 128)),
+        V((np_, nz, wh, 128)),
         V((np_, ph, 128)), V((np_, ph, 128)), V((ph, 128)), V((nz, ph, 128)), V((ph, 128)), V((np_, ph, 128)),
-        D((9,)), D((2, nz)), D((2, nz)), D((3, nq)), D((3, nq)), D((4, np_)), D((4, np_)), D((3, na)), D((3, na)),
+        D((9,)), D((5, nz)), D((5, nz)), D((8, np_)), D((8, np_)),
     ]
     outs = pl.pallas_call(
         functools.partial(main_kernel, dims),
@@ -435,7 +423,7 @@
     return tuple(r.T if i == 4 else r for i, r in enumerate(results))
 
 
-DIMS = (2, 4, 4, 4)
+DIMS = (2, 16, 4)
 
 
 def solution(mesh, dims=DIMS):

time: 81.4 us -> 69.4 us (0.85)
  Pallas kernels: 80.2 us -> 68.5 us
    pallas_call x1, Pallas kernels: 78.5 us -> 66.8 us  [local(): pl.pallas_call(functools.partial(main_kernel, dims), out_shape=[jax.Shape...]
where the time goes in v3:
time: 69.4 us; the launch traced here: 69.1 us
  Pallas kernels  68.5 us (99%)
    pallas_call x1, Pallas kernels, local(): pl.pallas_call(functools.partial(main_kernel, dims), out_shape=[jax.Shape...  66.8 us
    pallas_call x1, Pallas kernels, local(): pl.pallas_call(final_kernel, out_shape=[jax.ShapeDtypeStruct(pair.shape,...  1.71 us

profile of v3, /device:TPU:24, one launch (start us, length us, event | category | flops | bytes accessed | tf_op | source)
XLA Modules:
  0.0 69.1 jit_solution(4553890057095043006)
XLA Ops:
  0.6 66.8 %shard_map.144 = (bf16[2,256,128]{2,1,0:T(8,128)(2,1)S(1)}, bf16[2,256,128]{2,1,0:T(8,128)(2,1)S(1)}, bf16[64,256]{1,0:T(8,128)(2,1)S(1)}, bf16[2048,128]{1,0:T(8,128)(2,1)S(1)}, bf16[128,128]{1,0:T(8,128)(2,1)S(1)}) custom-call(bf16[32,2,256]{2,1,0:T(2,128)(2,1)} %msa_hbm.1, bf16[2,256,128]{2,1,0:T(8,128)(2,1)} %pair_hbm.1, bf16[2,256,128]{2,1,0:T(8,128)(2,1)} %cot_hbm.1, ...), custom_call_target="tpu_custom_call" | custom-call | tf_op jit(solution)/shard_map/pallas_call | solution.py:388
  67.4 1.7 %shard_map.145 = (bf16[2,256,128]{2,1,0:T(8,128)(2,1)}, bf16[2,256,128]{2,1,0:T(8,128)(2,1)}, bf16[32,2,256]{2,1,0:T(2,128)(2,1)}, f32[1024,128]{1,0:T(8,128)}, ...) custom-call(bf16[2,256,128]{2,1,0:T(8,128)(2,1)S(1)} %get-tuple-element.19.pair_in, ...), custom_call_target="tpu_custom_call" | custom-call | tf_op jit(solution)/shard_map/pallas_call | solution.py:407

commit v4 on v3

--- a/solution.py
+++ b/solution.py
@@ -77,9 +77,6 @@
             ]
         )
     ]
-    for load in loads[0:3]:
-        load.start()
-
     def far_first(i):
         return lax.rem(z + nz // 2 + (1 - 2 * lax.rem(i, 2)) * ((i + 1) // 2), nz)
 
@@ -88,6 +85,9 @@
     @pl.loop(0, nz - 1)
     def _(i):
         pl.semaphore_signal(barrier, inc=1, device_id=z_device(far_first(i)), device_id_type=MESH)
+
+    for load in loads[0:3]:
+        load.start()
 
     @pl.loop(1, np_)
     def _(k):
@@ -110,8 +110,8 @@
                 send_sem=self.send.at[self.stage, to], recv_sem=self.recv.at[self.stage, slot],
                 device_id=self.device(to), device_id_type=MESH)
 
-        def start(self):
-            @pl.loop(1, self.count)
+        def start(self, first=1, last=None):
+            @pl.loop(first, self.count if last is None else last)
             def _(i):
                 to = self.peer(i)
                 self.copy(to, self.mine, self.dst(to, self.mine)).start()
@@ -139,10 +139,14 @@
     x_far = Exchange(
         "xy", 1, lambda to: gathered.at[y, near:nz, x],
         lambda _, s: gathered.at[s // nx, near:nz, lax.rem(s, nx)])
-    x_d = Exchange("xy", 2, lambda to: d_part.at[to // nx, :, lax.rem(to, nx)], lambda _, s: d_recv.at[s])
-    x_d2 = Exchange("z", 1, lambda to: d_mid.at[to], lambda _, s: d_recv2.at[s])
-    x_w = Exchange("xy", 3, lambda to: w_part.at[to], lambda _, s: w_recv.at[s])
-    x_w2 = Exchange("z", 2, lambda to: w_mid.at[to], lambda _, s: w_recv2.at[s])
+    x_d_far = Exchange(
+        "xy", 2, lambda to: d_part.at[to // nx, near:nz, lax.rem(to, nx)], lambda _, s: d_recv.at[s, near:nz])
+    x_d_near = Exchange(
+        "xy", 8, lambda to: d_part.at[to // nx, 0:near, lax.rem(to, nx)], lambda _, s: d_recv.at[s, 0:near])
+    x_d2 = Exchange("z", 1, lambda to: d_mid.at[slot_of(z, to)], lambda _, s: d_recv2.at[s])
+    x_w1_far = Exchange("xy", 3, lambda to: w_part.at[to, near:nz], lambda _, s: w_recv.at[s, near:nz])
+    x_w1_near = Exchange("xy", 9, lambda to: w_part.at[to, 0:near], lambda _, s: w_recv.at[s, 0:near])
+    x_w2 = Exchange("z", 2, lambda to: w_mid.at[slot_of(z, to)], lambda _, s: w_recv2.at[s])
     x_w3 = Exchange("z", 3, lambda to: w_own, lambda at_z, s: w_all.at[p, slot_of(at_z, s)])
     x_w_near = Exchange("xy", 4, lambda to: w_all.at[p, 0:near], lambda _, s: w_all.at[s, 0:near])
     x_w_far = Exchange("xy", 5, lambda to: w_all.at[p, near:nz], lambda _, s: w_all.at[s, near:nz])
@@ -150,10 +154,10 @@
     x_p2 = Exchange("z", 4, lambda to: p_mid, lambda _, s: p_recv2.at[s])
     x_p3 = Exchange("xy", 7, lambda to: p_own, lambda _, s: p_all.at[s])
 
-    def summed(ref, count):
-        total = ref[0].astype(F32)
+    def summed(ref, count, first=None, last=None):
+        total = ref[0, first:last].astype(F32)
         for i in range(1, count):
-            total += ref[i].astype(F32)
+            total += ref[i, first:last].astype(F32)
         return total
 
     for load in loads[0:3]:
@@ -231,8 +235,11 @@
 
     for g in range(8):
         flat[pl.ds(g, 2 * n, stride=8), :] = dot(g_mat[...], m_mat[g * 128 : (g + 1) * 128, :], 1, 1)
-    d_part[...] = flat[...].astype(BF16).reshape(d_part.shape)
-    x_d.start()
+    for zz in range(nz):
+        for yy in range(ny):
+            block = flat[(yy * nz + zz) * nx * 16 : (yy * nz + zz + 1) * nx * 16, :].astype(BF16)
+            d_part[yy, slot_of(z, zz)] = block.reshape(nx, 16, 128)
+    x_d_far.start()
 
     for block in range(8):
         dm = dot(r_mat[:, block * 128 : (block + 1) * 128], g_mat[...], 0, 0)
@@ -246,7 +253,7 @@
     def put(first, value):
         for i in range(0, value.shape[0], 16):
             peer, row = divmod(first + i, slab)
-            w_part[peer, row // height, row % height : row % height + 16] = value[i : i + 16].astype(BF16)
+            w_part[peer, slot_of(z, row // height), row % height : row % height + 16] = value[i : i + 16].astype(BF16)
 
     for block in range(4):
         go = dot(left_t[...], dm_wide[:, block * 1024 : (block + 1) * 1024]) * (1.0 / 32.0)
@@ -256,6 +263,7 @@
     up = dot(pn[0], d_pre[0], 0, 0) + dot(pn[1], d_pre[1], 0, 0)
     for i in range(4):
         put(1536 + i * 128, up[:, i * 128 : (i + 1) * 128])
+    x_w1_far.start()
     d_left_t = (dot(wide[...], dm_wide[...], 1, 1) * (1.0 / 32.0)).astype(BF16)
 
     def transposed(block):
@@ -269,17 +277,23 @@
 
     d_recv[p] = d_part[y, :, x]
     w_recv[p] = w_part[p]
-    x_d.wait()
-    total = summed(d_recv, np_).astype(BF16)
-    d_mid[...] = total
-    x_d2.start()
-    x_w.start()
-    d_recv2[z] = d_mid[z]
-
-    x_w.wait()
-    w_mid[...] = summed(w_recv, np_).astype(BF16)
-    x_w2.start()
-    w_recv2[z] = w_mid[z]
+    far_end = nz - 2 * half
+    x_d_far.wait()
+    d_mid[near:nz] = summed(d_recv, np_, near, nz).astype(BF16)
+    x_d2.start(1, far_end)
+    x_d_near.start()
+    x_w1_far.wait()
+    w_mid[near:nz] = summed(w_recv, np_, near, nz).astype(BF16)
+    x_w2.start(1, far_end)
+    x_w1_near.start()
+    x_d_near.wait()
+    d_mid[0:near] = summed(d_recv, np_, 0, near).astype(BF16)
+    x_d2.start(far_end)
+    d_recv2[z] = d_mid[half]
+    x_w1_near.wait()
+    w_mid[0:near] = summed(w_recv, np_, 0, near).astype(BF16)
+    x_w2.start(far_end)
+    w_recv2[z] = w_mid[half]
 
     x_d2.wait()
     d_proj_t = jnp.concatenate([d_left_t, transposed(summed(d_recv2, nz))], axis=0)
@@ -298,7 +312,7 @@
     x_p2.start()
     p_recv2[z] = total
 
-    for plan in (x_z, x_near, x_far, x_d, x_w):
+    for plan in (x_z, x_near, x_far, x_d_far, x_w1_far, x_d_near, x_w1_near):
         plan.done()
 
     x_w2.wait()
@@ -383,7 +397,7 @@
         V((np_, nz, wh, 128)), V((np_, nz, wh, 128)), V((nz, wh, 128)), V((nz, wh, 128)), V((wh, 128)),
         V((np_, nz, wh, 128)),
         V((np_, ph, 128)), V((np_, ph, 128)), V((ph, 128)), V((nz, ph, 128)), V((ph, 128)), V((np_, ph, 128)),
-        D((9,)), D((5, nz)), D((5, nz)), D((8, np_)), D((8, np_)),
+        D((9,)), D((5, nz)), D((5, nz)), D((10, np_)), D((10, np_)),
     ]
     outs = pl.pallas_call(
         functools.partial(main_kernel, dims),

time: 69.4 us -> 69.8 us (level)
  no operation moved by 1% of the time
where the time goes in v4:
time: 69.8 us; the launch traced here: 69.3 us
  Pallas kernels  68.7 us (98%)
    pallas_call x1, Pallas kernels, local(): pl.pallas_call(functools.partial(main_kernel, dims), out_shape=[jax.Shape...  67 us
    pallas_call x1, Pallas kernels, local(): pl.pallas_call(final_kernel, out_shape=[jax.ShapeDtypeStruct(pair.shape,...  1.71 us

profile of v4, /device:TPU:24, one launch (start us, length us, event | category | flops | bytes accessed | tf_op | source)
XLA Modules:
  0.0 69.3 jit_solution(2424830371259481689)
XLA Ops:
  0.6 67.0 %shard_map.144 = (bf16[2,256,128]{2,1,0:T(8,128)(2,1)S(1)}, bf16[2,256,128]{2,1,0:T(8,128)(2,1)S(1)}, bf16[64,256]{1,0:T(8,128)(2,1)S(1)}, bf16[2048,128]{1,0:T(8,128)(2,1)S(1)}, bf16[128,128]{1,0:T(8,128)(2,1)S(1)}) custom-call(bf16[32,2,256]{2,1,0:T(2,128)(2,1)} %msa_hbm.1, bf16[2,256,128]{2,1,0:T(8,128)(2,1)} %pair_hbm.1, bf16[2,256,128]{2,1,0:T(8,128)(2,1)} %cot_hbm.1, ...), custom_call_target="tpu_custom_call" | custom-call | tf_op jit(solution)/shard_map/pallas_call | solution.py:402
  67.6 1.7 %shard_map.145 = (bf16[2,256,128]{2,1,0:T(8,128)(2,1)}, bf16[2,256,128]{2,1,0:T(8,128)(2,1)}, bf16[32,2,256]{2,1,0:T(2,128)(2,1)}, f32[1024,128]{1,0:T(8,128)}, ...) custom-call(bf16[2,256,128]{2,1,0:T(8,128)(2,1)S(1)} %get-tuple-element.19.pair_in, ...), custom_call_target="tpu_custom_call" | custom-call | tf_op jit(solution)/shard_map/pallas_call | solution.py:421

commit v5 on v4

--- a/solution.py
+++ b/solution.py
@@ -263,7 +263,7 @@
     up = dot(pn[0], d_pre[0], 0, 0) + dot(pn[1], d_pre[1], 0, 0)
     for i in range(4):
         put(1536 + i * 128, up[:, i * 128 : (i + 1) * 128])
-    x_w1_far.start()
+    x_d_near.start()
     d_left_t = (dot(wide[...], dm_wide[...], 1, 1) * (1.0 / 32.0)).astype(BF16)
 
     def transposed(block):
@@ -281,19 +281,15 @@
     x_d_far.wait()
     d_mid[near:nz] = summed(d_recv, np_, near, nz).astype(BF16)
     x_d2.start(1, far_end)
-    x_d_near.start()
+    x_w1_far.start()
+    x_d_near.wait()
+    d_mid[0:near] = summed(d_recv, np_, 0, near).astype(BF16)
+    x_d2.start(far_end)
+    x_w1_near.start()
+    d_recv2[z] = d_mid[half]
     x_w1_far.wait()
     w_mid[near:nz] = summed(w_recv, np_, near, nz).astype(BF16)
     x_w2.start(1, far_end)
-    x_w1_near.start()
-    x_d_near.wait()
-    d_mid[0:near] = summed(d_recv, np_, 0, near).astype(BF16)
-    x_d2.start(far_end)
-    d_recv2[z] = d_mid[half]
-    x_w1_near.wait()
-    w_mid[0:near] = summed(w_recv, np_, 0, near).astype(BF16)
-    x_w2.start(far_end)
-    w_recv2[z] = w_mid[half]
 
     x_d2.wait()
     d_proj_t = jnp.concatenate([d_left_t, transposed(summed(d_recv2, nz))], axis=0)
@@ -301,6 +297,12 @@
     pwg = jnp.concatenate([pwg[:, 0:128], pwg[:, 128:256]], axis=0).astype(BF16)
     p_part[...] = pwg.reshape(p_part.shape)
     x_p.start()
+
+    x_w1_near.wait()
+    w_mid[0:near] = summed(w_recv, np_, 0, near).astype(BF16)
+    x_w2.start(far_end)
+    w_recv2[z] = w_mid[half]
+
     p_recv[p] = p_part[p]
     d_norm = dot(d_proj_t, wp_ref[...], 0, 0)
     slope = layer_norm_adjoint(d_norm, gm_ref[...], unit_m[...], scale_m[:, 0:1])

time: 69.8 us -> 68.7 us (0.984)
  Pallas kernels: 68.7 us -> 67.5 us
    pallas_call x1, Pallas kernels: 67 us -> 65.8 us  [local(): pl.pallas_call(functools.partial(main_kernel, dims), out_shape=[jax.Shape...]
where the time goes in v5:
time: 68.7 us; the launch traced here: 68.1 us
  Pallas kernels  67.5 us (98%)
    pallas_call x1, Pallas kernels, local(): pl.pallas_call(functools.partial(main_kernel, dims), out_shape=[jax.Shape...  65.8 us
    pallas_call x1, Pallas kernels, local(): pl.pallas_call(final_kernel, out_shape=[jax.ShapeDtypeStruct(pair.shape,...  1.71 us

profile of v5, /device:TPU:24, one launch (start us, length us, event | category | flops | bytes accessed | tf_op | source)
XLA Modules:
  0.0 68.1 jit_solution(2337696799468728928)
XLA Ops:
  0.6 65.8 %shard_map.144 = (bf16[2,256,128]{2,1,0:T(8,128)(2,1)S(1)}, bf16[2,256,128]{2,1,0:T(8,128)(2,1)S(1)}, bf16[64,256]{1,0:T(8,128)(2,1)S(1)}, bf16[2048,128]{1,0:T(8,128)(2,1)S(1)}, bf16[128,128]{1,0:T(8,128)(2,1)S(1)}) custom-call(bf16[32,2,256]{2,1,0:T(2,128)(2,1)} %msa_hbm.1, bf16[2,256,128]{2,1,0:T(8,128)(2,1)} %pair_hbm.1, bf16[2,256,128]{2,1,0:T(8,128)(2,1)} %cot_hbm.1, ...), custom_call_target="tpu_custom_call" | custom-call | tf_op jit(solution)/shard_map/pallas_call | solution.py:404
  66.4 1.7 %shard_map.145 = (bf16[2,256,128]{2,1,0:T(8,128)(2,1)}, bf16[2,256,128]{2,1,0:T(8,128)(2,1)}, bf16[32,2,256]{2,1,0:T(2,128)(2,1)}, f32[1024,128]{1,0:T(8,128)}, ...) custom-call(bf16[2,256,128]{2,1,0:T(8,128)(2,1)S(1)} %get-tuple-element.19.pair_in, ...), custom_call_target="tpu_custom_call" | custom-call | tf_op jit(solution)/shard_map/pallas_call | solution.py:423

commit v6 on v5

--- a/solution.py
+++ b/solution.py
@@ -82,14 +82,14 @@
 
     barrier = pltpu.get_barrier_semaphore()
 
-    @pl.loop(0, nz - 1)
+    @pl.loop(0, nz - 1, unroll=True)
     def _(i):
         pl.semaphore_signal(barrier, inc=1, device_id=z_device(far_first(i)), device_id_type=MESH)
 
     for load in loads[0:3]:
         load.start()
 
-    @pl.loop(1, np_)
+    @pl.loop(1, np_, unroll=True)
     def _(k):
         pl.semaphore_signal(barrier, inc=1, device_id=xy_device(lax.rem(p + k, np_)), device_id_type=MESH)
 
@@ -111,19 +111,19 @@
                 device_id=self.device(to), device_id_type=MESH)
 
         def start(self, first=1, last=None):
-            @pl.loop(first, self.count if last is None else last)
+            @pl.loop(first, self.count if last is None else last, unroll=True)
             def _(i):
                 to = self.peer(i)
                 self.copy(to, self.mine, self.dst(to, self.mine)).start()
 
         def wait(self, first=1, last=None):
-            @pl.loop(first, self.count if last is None else last)
+            @pl.loop(first, self.count if last is None else last, unroll=True)
             def _(i):
                 slot = self.peer(i)
                 self.copy(slot, slot, self.dst(self.mine, slot)).wait_recv()
 
         def done(self):
-            @pl.loop(1, self.count)
+            @pl.loop(1, self.count, unroll=True)
             def _(i):
                 to = self.peer(i)
                 self.copy(to, to, self.dst(self.mine, to)).wait_send()

time: 68.7 us -> 67.6 us (0.984)
  Pallas kernels: 67.5 us -> 66.3 us
    pallas_call x1, Pallas kernels: 65.8 us -> 64.6 us  [local(): pl.pallas_call(functools.partial(main_kernel, dims), out_shape=[jax.Shape...]
where the time goes in v6:
time: 67.6 us; the launch traced here: 67 us
  Pallas kernels  66.3 us (98%)
    pallas_call x1, Pallas kernels, local(): pl.pallas_call(functools.partial(main_kernel, dims), out_shape=[jax.Shape...  64.6 us
    pallas_call x1, Pallas kernels, local(): pl.pallas_call(final_kernel, out_shape=[jax.ShapeDtypeStruct(pair.shape,...  1.71 us

profile of v6, /device:TPU:24, one launch (start us, length us, event | category | flops | bytes accessed | tf_op | source)
XLA Modules:
  0.0 67.0 jit_solution(12906554114299524660)
XLA Ops:
  0.6 64.6 %shard_map.144 = (bf16[2,256,128]{2,1,0:T(8,128)(2,1)S(1)}, bf16[2,256,128]{2,1,0:T(8,128)(2,1)S(1)}, bf16[64,256]{1,0:T(8,128)(2,1)S(1)}, bf16[2048,128]{1,0:T(8,128)(2,1)S(1)}, bf16[128,128]{1,0:T(8,128)(2,1)S(1)}) custom-call(bf16[32,2,256]{2,1,0:T(2,128)(2,1)} %msa_hbm.1, bf16[2,256,128]{2,1,0:T(8,128)(2,1)} %pair_hbm.1, bf16[2,256,128]{2,1,0:T(8,128)(2,1)} %cot_hbm.1, ...), custom_call_target="tpu_custom_call" | custom-call | tf_op jit(solution)/shard_map/pallas_call | solution.py:404
  65.3 1.7 %shard_map.145 = (bf16[2,256,128]{2,1,0:T(8,128)(2,1)}, bf16[2,256,128]{2,1,0:T(8,128)(2,1)}, bf16[32,2,256]{2,1,0:T(2,128)(2,1)}, f32[1024,128]{1,0:T(8,128)}, ...) custom-call(bf16[2,256,128]{2,1,0:T(8,128)(2,1)S(1)} %get-tuple-element.19.pair_in, ...), custom_call_target="tpu_custom_call" | custom-call | tf_op jit(solution)/shard_map/pallas_call | solution.py:423

commit v7 on v6

--- a/solution.py
+++ b/solution.py
@@ -314,14 +314,13 @@
     x_p2.start()
     p_recv2[z] = total
 
-    for plan in (x_z, x_near, x_far, x_d_far, x_w1_far, x_d_near, x_w1_near):
-        plan.done()
-
     x_w2.wait()
     total = summed(w_recv2, nz).astype(BF16)
     w_own[...] = total
     x_w3.start()
     w_all[p, half] = total
+    for plan in (x_z, x_near, x_far, x_d_far, x_w1_far, x_d_near, x_w1_near):
+        plan.done()
 
     x_w3.wait(nz - 2 * half)
     x_w_near.start()

time: 67.6 us -> 67.6 us (level)
  no operation moved by 1% of the time
where the time goes in v7:
time: 67.6 us; the launch traced here: 67 us
  Pallas kernels  66.3 us (98%)
    pallas_call x1, Pallas kernels, local(): pl.pallas_call(functools.partial(main_kernel, dims), out_shape=[jax.Shape...  64.6 us
    pallas_call x1, Pallas kernels, local(): pl.pallas_call(final_kernel, out_shape=[jax.ShapeDtypeStruct(pair.shape,...  1.71 us

profile of v7, /device:TPU:24, one launch (start us, length us, event | category | flops | bytes accessed | tf_op | source)
XLA Modules:
  0.0 67.0 jit_solution(10470311481864924332)
XLA Ops:
  0.6 64.6 %shard_map.144 = (bf16[2,256,128]{2,1,0:T(8,128)(2,1)S(1)}, bf16[2,256,128]{2,1,0:T(8,128)(2,1)S(1)}, bf16[64,256]{1,0:T(8,128)(2,1)S(1)}, bf16[2048,128]{1,0:T(8,128)(2,1)S(1)}, bf16[128,128]{1,0:T(8,128)(2,1)S(1)}) custom-call(bf16[32,2,256]{2,1,0:T(2,128)(2,1)} %msa_hbm.1, bf16[2,256,128]{2,1,0:T(8,128)(2,1)} %pair_hbm.1, bf16[2,256,128]{2,1,0:T(8,128)(2,1)} %cot_hbm.1, ...), custom_call_target="tpu_custom_call" | custom-call | tf_op jit(solution)/shard_map/pallas_call | solution.py:403
  65.3 1.7 %shard_map.145 = (bf16[2,256,128]{2,1,0:T(8,128)(2,1)}, bf16[2,256,128]{2,1,0:T(8,128)(2,1)}, bf16[32,2,256]{2,1,0:T(2,128)(2,1)}, f32[1024,128]{1,0:T(8,128)}, ...) custom-call(bf16[2,256,128]{2,1,0:T(8,128)(2,1)S(1)} %get-tuple-element.19.pair_in, ...), custom_call_target="tpu_custom_call" | custom-call | tf_op jit(solution)/shard_map/pallas_call | solution.py:422

commit v8 on v6

--- a/solution.py
+++ b/solution.py
@@ -240,6 +240,7 @@
             block = flat[(yy * nz + zz) * nx * 16 : (yy * nz + zz + 1) * nx * 16, :].astype(BF16)
             d_part[yy, slot_of(z, zz)] = block.reshape(nx, 16, 128)
     x_d_far.start()
+    x_d_near.start()
 
     for block in range(8):
         dm = dot(r_mat[:, block * 128 : (block + 1) * 128], g_mat[...], 0, 0)
@@ -263,7 +264,6 @@
     up = dot(pn[0], d_pre[0], 0, 0) + dot(pn[1], d_pre[1], 0, 0)
     for i in range(4):
         put(1536 + i * 128, up[:, i * 128 : (i + 1) * 128])
-    x_d_near.start()
     d_left_t = (dot(wide[...], dm_wide[...], 1, 1) * (1.0 / 32.0)).astype(BF16)
 
     def transposed(block):

time: 67.6 us -> 67.3 us (level)
  no operation moved by 1% of the time
where the time goes in v8:
time: 67.3 us; the launch traced here: 66.7 us
  Pallas kernels  66.1 us (98%)
    pallas_call x1, Pallas kernels, local(): pl.pallas_call(functools.partial(main_kernel, dims), out_shape=[jax.Shape...  64.4 us
    pallas_call x1, Pallas kernels, local(): pl.pallas_call(final_kernel, out_shape=[jax.ShapeDtypeStruct(pair.shape,...  1.71 us

profile of v8, /device:TPU:24, one launch (start us, length us, event | category | flops | bytes accessed | tf_op | source)
XLA Modules:
  0.0 66.7 jit_solution(4210947047553872507)
XLA Ops:
  0.6 64.4 %shard_map.144 = (bf16[2,256,128]{2,1,0:T(8,128)(2,1)S(1)}, bf16[2,256,128]{2,1,0:T(8,128)(2,1)S(1)}, bf16[64,256]{1,0:T(8,128)(2,1)S(1)}, bf16[2048,128]{1,0:T(8,128)(2,1)S(1)}, bf16[128,128]{1,0:T(8,128)(2,1)S(1)}) custom-call(bf16[32,2,256]{2,1,0:T(2,128)(2,1)} %msa_hbm.1, bf16[2,256,128]{2,1,0:T(8,128)(2,1)} %pair_hbm.1, bf16[2,256,128]{2,1,0:T(8,128)(2,1)} %cot_hbm.1, ...), custom_call_target="tpu_custom_call" | custom-call | tf_op jit(solution)/shard_map/pallas_call | solution.py:404
  65.0 1.7 %shard_map.145 = (bf16[2,256,128]{2,1,0:T(8,128)(2,1)}, bf16[2,256,128]{2,1,0:T(8,128)(2,1)}, bf16[32,2,256]{2,1,0:T(2,128)(2,1)}, f32[1024,128]{1,0:T(8,128)}, ...) custom-call(bf16[2,256,128]{2,1,0:T(8,128)(2,1)S(1)} %get-tuple-element.19.pair_in, ...), custom_call_target="tpu_custom_call" | custom-call | tf_op jit(solution)/shard_map/pallas_call | solution.py:423
